TPU v7x, 32 devices: a whole 2x2x4 slice. The times are simulated.
32 devices in a mesh: dp: 8 (over y, x, core), tensor: 4 (over z).
Axes of the slice: x: 2, y: 2, z: 4, core: 2. Of those that a mesh axis runs over, the one named last changes fastest.
Arguments:
- tokens: bfloat16 [16384, 1024], P(('dp', 'tensor')), may hold values from -6 to 6
- cotangent: bfloat16 [16384, 1024], P(('dp', 'tensor')), may hold values from -6 to 6
- segments: int32 [16384], P('dp'), may hold values from 0 to 18, as said below
- attn_w: float32 [4, 1024, 1024], P(None, 'dp', 'tensor')
- mlp_w: float32 [2, 1024, 4096], P(None, 'dp', 'tensor')
- vectors: float32 [12, 1024], replicated
- attn_mom: float32 [4, 1024, 1024], P(None, 'dp', 'tensor')
- mlp_mom: float32 [2, 1024, 4096], P(None, 'dp', 'tensor')
- vector_mom: float32 [12, 1024], replicated, may hold values from -768 to 768
Outputs:
- block_out: bfloat16 [16384, 1024], P(('dp', 'tensor'))
- dx: float32 [16384, 1024], P(('dp', 'tensor'))
- attn_mom_new: float32 [4, 1024, 1024], P(None, 'dp', 'tensor')
- attn_new: float32 [4, 1024, 1024], P(None, 'dp', 'tensor')
- mlp_mom_new: float32 [2, 1024, 4096], P(None, 'dp', 'tensor')
- mlp_new: float32 [2, 1024, 4096], P(None, 'dp', 'tensor')
- vector_mom_new: float32 [12, 1024], replicated
- vector_new: float32 [12, 1024], replicated
Inputs may be any that keep to these rules, and one draw needn't show every extreme that they name: `segments`: within each sequence of 1024 tokens the ids above zero never fall; an id above zero is one document of 60 to 800 tokens, the last document of a sequence possibly cut shorter, and the last document of every sequence has the id 1024 // 60 + 1; zero marks padding of fewer than 60 tokens at a sequence's end.
All inputs are finite; a program needn't handle non-finite values.
Results may differ from a plain program's by a relative error of at most 0.033.
Values may be sent and summed in bfloat16 or wider, within the bound.
A program may use at most 128 MiB of HBM per device.

v0:
```python
import functools
import math

import jax
import jax.numpy as jnp
from jax import lax
from jax.experimental import pallas as pl
from jax.experimental.pallas import tpu as pltpu
from jax.sharding import PartitionSpec as P

D = 1024
HEADS = 16
HD = 64
FF = 4096
SEQ = 1024
NS_STEPS = 5
MESH = pl.DeviceIdType.MESH


coeff_a = 3.4445
coeff_b = -4.775
coeff_c = 2.0315


def norm_rows(row_data, gain, shift):
    center = jnp.mean(row_data, axis=-1, keepdims=True)
    centred = row_data - center
    spread = jnp.mean(centred * centred, axis=-1, keepdims=True)
    return centred * lax.rsqrt(spread + 1e-05) * gain + shift


def gelu_tanh(values):
    return jax.nn.gelu(values, approximate=True)


def contract_last(left, right):
    return lax.dot_general(
        left, right, (((1,), (1,)), ((), ())), preferred_element_type=jnp.float32
    )


def contract_first(left, right):
    return lax.dot_general(
        left, right, (((0,), (0,)), ((), ())), preferred_element_type=jnp.float32
    )


def head_slopes(first_head, head_count):
    head_ids = (first_head + jnp.arange(head_count)).astype(jnp.float32)
    return jnp.exp2(-(8.0 / HEADS) * (head_ids + 1.0))


def masked_scores(row_query, key_rows, row_segs, seg_ids, row_start, slopes):
    scores = jnp.einsum("qhd,khd->hqk", row_query, key_rows, preferred_element_type=jnp.float32) * (
        1.0 / math.sqrt(HD)
    )
    query_pos = row_start + jnp.arange(row_query.shape[0])
    key_pos = jnp.arange(key_rows.shape[0])
    distance = (query_pos[:, None] - key_pos[None, :]).astype(jnp.float32)
    scores = scores - slopes[:, None, None] * distance[None]
    same_doc = (
        (row_segs[:, None] == seg_ids[None, :])
        & (row_segs[:, None] > 0)
        & (key_pos[None, :] <= query_pos[:, None])
    )
    allowed = same_doc | (key_pos[None, :] == query_pos[:, None])
    return jnp.where(allowed[None], scores, -1e30)


def attend_forward(query, key_rows, value_rows, seg_ids, slopes, row_block):
    length = key_rows.shape[0]

    def one_block(row_start):
        row_query = lax.dynamic_slice_in_dim(query, row_start, row_block, 0)
        row_segs = lax.dynamic_slice_in_dim(seg_ids, row_start, row_block, 0)
        scores = masked_scores(row_query, key_rows, row_segs, seg_ids, row_start, slopes)
        row_max = jnp.max(scores, axis=-1, keepdims=True)
        exp_scores = jnp.exp(scores - row_max)
        row_total = jnp.sum(exp_scores, axis=-1, keepdims=True)
        attn_probs = (exp_scores / row_total).astype(jnp.bfloat16)
        mixed = jnp.einsum(
            "hqk,khd->qhd", attn_probs, value_rows, preferred_element_type=jnp.float32
        )
        return (mixed.astype(jnp.bfloat16), (row_max + jnp.log(row_total))[..., 0])

    block_starts = jnp.arange(length // row_block) * row_block
    mixed, log_sums = lax.map(one_block, block_starts)
    return (mixed.reshape(length, -1), log_sums)


def attend_backward(query, key_rows, value_rows, seg_ids, log_sums, grad_mixed, slopes, row_block):
    length, head_count, head_dim = key_rows.shape
    factor = 1.0 / math.sqrt(HD)

    def one_block(carry, pieces):
        row_start, row_lse = pieces
        row_query = lax.dynamic_slice_in_dim(query, row_start, row_block, 0)
        row_grad = lax.dynamic_slice_in_dim(grad_mixed, row_start, row_block, 0)
        row_segs = lax.dynamic_slice_in_dim(seg_ids, row_start, row_block, 0)
        scores = masked_scores(row_query, key_rows, row_segs, seg_ids, row_start, slopes)
        attn_probs = jnp.exp(scores - row_lse[:, :, None])
        grad_probs = jnp.einsum(
            "qhd,khd->hqk", row_grad, value_rows, preferred_element_type=jnp.float32
        )
        inner = jnp.sum(grad_probs * attn_probs, axis=-1, keepdims=True)
        grad_scores = (attn_probs * (grad_probs - inner)).astype(jnp.bfloat16)
        grad_query = (
            jnp.einsum("hqk,khd->qhd", grad_scores, key_rows, preferred_element_type=jnp.float32)
            * factor
        )
        grad_keys = (
            carry[0]
            + jnp.einsum("hqk,qhd->khd", grad_scores, row_query, preferred_element_type=jnp.float32)
            * factor
        )
        grad_values = carry[1] + jnp.einsum(
            "hqk,qhd->khd",
            attn_probs.astype(jnp.bfloat16),
            row_grad,
            preferred_element_type=jnp.float32,
        )
        return ((grad_keys, grad_values), grad_query)

    empty = jnp.zeros((length, head_count, head_dim), jnp.float32)
    block_starts = jnp.arange(length // row_block) * row_block
    (grad_keys, grad_values), grad_query = lax.scan(
        one_block, (empty, empty), (block_starts, log_sums)
    )
    return (
        grad_query.reshape(length, -1),
        grad_keys.reshape(length, -1),
        grad_values.reshape(length, -1),
    )


def newton_rows(row_iterate):
    for repeat in range(NS_STEPS + 1):
        whole_iterate = lax.all_gather(row_iterate, "tensor", axis=0, tiled=True)
        if repeat == NS_STEPS:
            break
        square_rows = contract_last(row_iterate, whole_iterate).astype(jnp.bfloat16)
        whole_square = lax.all_gather(square_rows, "tensor", axis=0, tiled=True)
        poly_rows = (
            coeff_b * square_rows.astype(jnp.float32)
            + coeff_c * jnp.dot(square_rows, whole_square, preferred_element_type=jnp.float32)
        ).astype(jnp.bfloat16)
        row_iterate = (
            coeff_a * row_iterate.astype(jnp.float32)
            + jnp.dot(poly_rows, whole_iterate, preferred_element_type=jnp.float32)
        ).astype(jnp.bfloat16)
    return whole_iterate


def on_device(tokens, cotangent, segments, attn_w, mlp_w, vectors, attn_mom, mlp_mom, vector_mom):
    tensor_size = lax.axis_size("tensor")
    dp_size = lax.axis_size("dp")
    tensor_index = lax.axis_index("tensor")
    dp_index = lax.axis_index("dp")
    row_count = tokens.shape[0]
    model_width = tokens.shape[1]
    local_width = attn_w.shape[2]
    local_hidden = mlp_w.shape[2]
    head_count = local_width // HD
    row_block = min(512, SEQ)
    total_tokens = row_count * tensor_size * dp_size
    gathered_attn, gathered_mlp = (
        lax.all_gather(attn_w.astype(jnp.bfloat16), "dp", axis=1, tiled=True),
        lax.all_gather(mlp_w.astype(jnp.bfloat16), "dp", axis=1, tiled=True),
    )
    hidden_bias = vectors[8:].reshape(-1)
    query_bias = lax.dynamic_slice_in_dim(vectors[2], tensor_index * local_width, local_width)
    value_bias = lax.dynamic_slice_in_dim(vectors[3], tensor_index * local_width, local_width)
    x_rows = tokens.astype(jnp.float32)
    normed, pull_first = jax.vjp(norm_rows, x_rows, vectors[0], vectors[1])
    all_normed = lax.all_gather(normed.astype(jnp.bfloat16), "tensor", axis=0, tiled=True)
    seq_count = all_normed.shape[0] // SEQ
    projected = jnp.einsum(
        "td,mdc->mtc", all_normed, gathered_attn[:3], preferred_element_type=jnp.float32
    )
    query = (projected[0] + query_bias).astype(jnp.bfloat16)
    key_rows = projected[1].astype(jnp.bfloat16)
    value_rows = (projected[2] + value_bias).astype(jnp.bfloat16)
    slopes = head_slopes(tensor_index * head_count, head_count)
    seq_shape = (seq_count, SEQ, head_count, HD)
    seq_segs = segments.reshape(seq_count, SEQ)

    def forward_seq(pieces):
        return attend_forward(pieces[0], pieces[1], pieces[2], pieces[3], slopes, row_block)

    mixed, log_sums = lax.map(
        forward_seq,
        (
            query.reshape(seq_shape),
            key_rows.reshape(seq_shape),
            value_rows.reshape(seq_shape),
            seq_segs,
        ),
    )
    mixed = mixed.reshape(-1, local_width)
    w_out = gathered_attn[3]
    middle = (
        x_rows
        + lax.psum_scatter(
            contract_last(mixed, w_out).astype(jnp.bfloat16),
            "tensor",
            scatter_dimension=0,
            tiled=True,
        ).astype(jnp.float32)
        + vectors[4]
    )
    hidden_normed, pull_second = jax.vjp(norm_rows, middle, vectors[5], vectors[6])
    hidden_low = hidden_normed.astype(jnp.bfloat16)
    grad_rows = cotangent.astype(jnp.float32)
    all_hidden = lax.all_gather(hidden_low, "tensor", axis=0, tiled=True)
    w_up = gathered_mlp[0]
    w_down = gathered_mlp[1]
    bias_local = lax.dynamic_slice_in_dim(hidden_bias, tensor_index * local_hidden, local_hidden)
    hidden_pre = jnp.dot(all_hidden, w_up, preferred_element_type=jnp.float32) + bias_local
    act_float, gelu_pull = jax.vjp(gelu_tanh, hidden_pre)
    hidden_act = act_float.astype(jnp.bfloat16)
    output = (
        middle
        + lax.psum_scatter(
            contract_last(hidden_act, w_down).astype(jnp.bfloat16),
            "tensor",
            scatter_dimension=0,
            tiled=True,
        ).astype(jnp.float32)
        + vectors[7]
    )
    all_grad = lax.all_gather(grad_rows.astype(jnp.bfloat16), "tensor", axis=0, tiled=True)
    grad_down = contract_first(all_grad, hidden_act)
    grad_act = jnp.dot(all_grad, w_down, preferred_element_type=jnp.float32)
    grad_pre = gelu_pull(grad_act)[0].astype(jnp.bfloat16)
    grad_up = contract_first(all_hidden, grad_pre)
    bias_part = jnp.sum(grad_pre, axis=0, dtype=jnp.float32)
    hidden_grad = lax.dynamic_update_slice_in_dim(
        jnp.zeros(hidden_bias.shape, jnp.float32), bias_part, tensor_index * local_hidden, 0
    )
    grad_hidden_in = lax.psum_scatter(
        contract_last(grad_pre, w_up).astype(jnp.bfloat16),
        "tensor",
        scatter_dimension=0,
        tiled=True,
    ).astype(jnp.float32)
    mlp_grads = jnp.stack([grad_up, grad_down])
    second_grads = pull_second(grad_hidden_in)
    grad_middle = grad_rows + second_grads[0]
    all_grad_mid = lax.all_gather(grad_middle.astype(jnp.bfloat16), "tensor", axis=0, tiled=True)
    grad_out_w = contract_first(all_grad_mid, mixed)
    grad_mixed = jnp.dot(all_grad_mid, w_out, preferred_element_type=jnp.float32).astype(
        jnp.bfloat16
    )

    def backward_seq(pieces):
        return attend_backward(
            pieces[0], pieces[1], pieces[2], pieces[3], pieces[4], pieces[5], slopes, row_block
        )

    grad_query, grad_keys, grad_values = lax.map(
        backward_seq,
        (
            query.reshape(seq_shape),
            key_rows.reshape(seq_shape),
            value_rows.reshape(seq_shape),
            seq_segs,
            log_sums,
            grad_mixed.reshape(seq_shape),
        ),
    )
    grad_qkv = (
        jnp.stack([grad_query, grad_keys, grad_values])
        .reshape(3, -1, local_width)
        .astype(jnp.bfloat16)
    )
    grad_proj_w = jnp.einsum(
        "td,mtc->mdc", all_normed, grad_qkv, preferred_element_type=jnp.float32
    )
    bias_sums = jnp.sum(grad_qkv, axis=1, dtype=jnp.float32)
    grad_normed = lax.psum_scatter(
        jnp.einsum(
            "mtc,mdc->td", grad_qkv, gathered_attn[:3], preferred_element_type=jnp.float32
        ).astype(jnp.bfloat16),
        "tensor",
        scatter_dimension=0,
        tiled=True,
    ).astype(jnp.float32)
    first_grads = pull_first(grad_normed)
    grad_tokens = grad_middle + first_grads[0]

    def placed(piece, full_size, offset):
        return lax.dynamic_update_slice_in_dim(
            jnp.zeros((full_size,), jnp.float32), piece, offset, 0
        )

    width_offset = tensor_index * local_width
    vector_rows = jnp.stack(
        [
            first_grads[1],
            first_grads[2],
            placed(bias_sums[0], model_width, width_offset),
            placed(bias_sums[2], model_width, width_offset),
            jnp.sum(grad_middle, axis=0),
            second_grads[1],
            second_grads[2],
            jnp.sum(grad_rows, axis=0),
        ]
    )
    vector_local = jnp.concatenate([vector_rows, hidden_grad.reshape(4, model_width)], axis=0)
    attn_grads = jnp.concatenate([grad_proj_w, grad_out_w[None]], axis=0)
    attn_sum, mlp_sum = (
        lax.psum_scatter(
            attn_grads.astype(jnp.bfloat16), "dp", scatter_dimension=1, tiled=True
        ).astype(jnp.float32),
        lax.psum_scatter(
            mlp_grads.astype(jnp.bfloat16), "dp", scatter_dimension=1, tiled=True
        ).astype(jnp.float32),
    )
    attn_mom_new = 0.5 * attn_mom + attn_sum
    mlp_mom_new = 0.5 * mlp_mom + mlp_sum
    attn_round = attn_mom_new.astype(jnp.bfloat16)
    mlp_round = mlp_mom_new.astype(jnp.bfloat16)
    attn_float = attn_round.astype(jnp.float32)
    mlp_float = mlp_round.astype(jnp.float32)
    norm_parts = jnp.concatenate(
        [jnp.sum(attn_float * attn_float, axis=(1, 2)), jnp.sum(mlp_float * mlp_float, axis=(1, 2))]
    )
    vector_grads, norm_sums = lax.psum((vector_local, norm_parts), ("dp", "tensor"))
    frob_norms = jnp.sqrt(norm_sums)
    owners = [order * dp_size // 6 for order in range(6)]
    owned_norm = jnp.zeros((), jnp.float32)
    for order in range(6):
        owned_norm = owned_norm + jnp.where(dp_index == owners[order], frob_norms[order], 0.0)
    block_rows = attn_w.shape[1]
    slice_rows = model_width // tensor_size
    full_cols = local_hidden * tensor_size
    rows_attn, rows_mlp = (
        lax.all_gather(attn_round, "tensor", axis=2, tiled=True),
        lax.all_gather(mlp_round, "tensor", axis=2, tiled=True),
    )
    padded_attn = jnp.pad(rows_attn, ((0, 0), (0, 0), (0, full_cols - model_width)))
    all_rows = jnp.concatenate([padded_attn, rows_mlp], axis=0)
    outgoing = jnp.zeros((dp_size, block_rows, full_cols), jnp.bfloat16)
    for order in range(6):
        outgoing = outgoing.at[owners[order]].set(all_rows[order])
    incoming = lax.all_to_all(outgoing, "dp", split_axis=0, concat_axis=0, tiled=True)
    owned_whole = incoming.reshape(model_width, full_cols)
    mine = lax.dynamic_slice_in_dim(owned_whole, tensor_index * slice_rows, slice_rows, 0)
    attn_col = tensor_index * local_width
    row_iterate = (mine.astype(jnp.float32) / (owned_norm + 1e-06)).astype(jnp.bfloat16)
    result = newton_rows(row_iterate)
    returned = lax.all_to_all(
        result.reshape(dp_size, block_rows, full_cols),
        "dp",
        split_axis=0,
        concat_axis=0,
        tiled=True,
    )
    attn_blocks = []
    for order in range(4):
        piece = lax.dynamic_slice_in_dim(returned[owners[order]], attn_col, local_width, 1)
        attn_blocks.append(attn_w[order] - piece.astype(jnp.float32))
    mlp_blocks = []
    for order in range(2):
        piece = lax.dynamic_slice_in_dim(
            returned[owners[4 + order]], tensor_index * local_hidden, local_hidden, 1
        )
        mlp_blocks.append(mlp_w[order] - math.sqrt(FF / D) * piece.astype(jnp.float32))
    attn_new = jnp.stack(attn_blocks)
    mlp_new = jnp.stack(mlp_blocks)
    vector_mom_new = 0.5 * vector_mom + vector_grads
    vector_new = vectors - 0.1 / math.sqrt(total_tokens) * vector_mom_new
    return (
        output.astype(jnp.bfloat16),
        grad_tokens,
        attn_mom_new,
        attn_new,
        mlp_mom_new,
        mlp_new,
        vector_mom_new,
        vector_new,
    )


CORES = 2


class Place:
    def __init__(self):
        self.dp = lax.axis_index("dp")
        self.tensor = lax.axis_index("tensor")
        self.line = lax.axis_size("tensor")
        self.devices = lax.axis_size("dp") * self.line
        self.me = self.dp * self.line + self.tensor
        self.core = lax.rem(self.dp, 2)
        self.chip = self.dp // 2
        self.x = lax.rem(self.chip, 2)
        self.y = self.chip // 2
        self.twin = (self.dp + 1 - 2 * self.core, self.tensor)
        self.across_x = (self.dp + 2 - 4 * self.x, self.tensor)
        self.across_y = (self.dp + 4 - 8 * self.y, self.tensor)
        self.right = (self.dp, self.tensor + 1)
        self.left = (self.dp, self.tensor - 1)
        self.stays = self.core == lax.rem(self.tensor, 2)
        self.corner = (self.dp + 1 - 2 * self.core, self.tensor - 1 + 2 * self.core)


    def of(self, index):
        return (index // self.line, lax.rem(index, self.line))

    def index(self, x, y, core, z):
        return ((2 * y + x) * 2 + core) * self.line + z


def greet(place, line):
    barrier = pltpu.get_barrier_semaphore()

    def signal(device):
        pl.semaphore_signal(barrier, inc=1, device_id=device, device_id_type=MESH)

    signal(place.twin)
    signal(place.across_x)
    signal(place.across_y)

    for other in range(line):

        @pl.when(place.tensor != other)
        def _():
            signal((place.dp, other))

    @pl.when(jnp.logical_not(place.stays))
    def _():
        signal(place.corner)

    pl.semaphore_wait(barrier, jnp.where(place.stays, 3 + line - 1, 3 + line))


OWNERS = ((1, 0, 0), (1, 0, 3), (0, 1, 0), (0, 1, 3), (0, 0, 1), (1, 1, 2))


def greet_all(place):
    barrier = pltpu.get_barrier_semaphore()

    def meet(step, carry):
        pl.semaphore_signal(
            barrier, inc=1, device_id=place.of(lax.rem(place.me + step, place.devices)), device_id_type=MESH
        )
        return carry

    lax.fori_loop(1, place.devices, meet, 0)
    pl.semaphore_wait(barrier, place.devices - 1)


def is_one_of(value, options):
    found = value < 0
    for option in options:
        found = found | (value == option)
    return found


def sides(order, line):
    oz = OWNERS[order][2]
    above, below = list(range(oz + 1, line)), list(range(oz))
    return (above, below) if len(above) > len(below) else (below, above)


def rows_held(place, whole, index, rows, width):
    dp, tensor = place.of(index)
    return whole.at[pl.ds(pl.multiple_of(dp * rows, rows), rows), columns(tensor * width, width)]


def remote(place, source, target, send, recv, index):
    return pltpu.make_async_remote_copy(
        src_ref=source,
        dst_ref=target,
        send_sem=send,
        recv_sem=recv,
        device_id=place.of(index),
        device_id_type=MESH,
    )


class Collect:
    @staticmethod
    def scratch():
        dma = pltpu.SemaphoreType.DMA
        return [dma((2, 2)), dma((1,)), dma((2, 2)), dma((2, 2))]

    SCRATCH = 4

    def __init__(self, place, source, whole, scratch):
        self.place, self.source, self.whole = place, source, whole
        self.send_sem, self.sem, self.pass_send, self.pass_recv = scratch
        self.rows, self.width = source.shape[1], source.shape[2] // 2

    def owner(self, order, half):
        ox, oy, oz = OWNERS[order]
        return self.place.index(ox, oy, half, oz)

    def piece(self, order, half):
        return self.source.at[order - 4, :, half * self.width : (half + 1) * self.width]

    def held(self, index):
        return rows_held(self.place, self.whole, index, self.rows, self.width)

    def direct(self, order, half):
        send = self.send_sem.at[order - 4, half]
        return remote(
            self.place, self.piece(order, half), self.held(self.place.me), send, self.sem.at[0], self.owner(order, half)
        )

    def own(self, order, half):
        return pltpu.make_async_copy(self.piece(order, half), self.held(self.place.me), self.sem.at[0])

    def by_way(self, order):
        place = self.place
        ox, oy, oz = OWNERS[order]
        lone = is_one_of(place.tensor, sides(order, place.line)[1])
        return (place.y != oy) & (place.tensor != oz) & ((place.x != ox) | lone)

    def to_way(self, order, half):
        place = self.place
        ox, oy, _ = OWNERS[order]
        which = jnp.where(place.x == ox, 1, 0)
        return remote(
            place,
            self.piece(order, half),
            self.held(place.me),
            self.send_sem.at[order - 4, half],
            self.pass_recv.at[which, place.core],
            place.index(ox, oy, half, place.tensor),
        )

    def passed(self, order, which, cores):
        ox, oy, _ = OWNERS[order]
        return self.place.index(1 - ox if which == 0 else ox, 1 - oy, cores, self.place.tensor)

    def pass_in(self, order, which, cores):
        index = self.passed(order, which, cores)
        region = self.held(index)
        sems = self.pass_send.at[which, cores], self.pass_recv.at[which, cores]
        return remote(self.place, region, region, *sems, index)

    def pass_on(self, order, which, cores):
        ox, oy, oz = OWNERS[order]
        region = self.held(self.passed(order, which, cores))
        owner = self.place.index(ox, oy, self.place.core, oz)
        return remote(self.place, region, region, self.pass_send.at[which, cores], self.sem.at[0], owner)

    def when_passing(self, action):
        place = self.place
        for order in (5, 4):
            ox, oy, _ = OWNERS[order]
            far, lone = sides(order, place.line)
            for which, planes in ((0, far + lone), (1, lone)):

                @pl.when((place.x == ox) & (place.y == oy) & is_one_of(place.tensor, planes))
                def _():
                    for cores in range(2):
                        action(order, which, cores)

    def each(self, action_way, action_direct, action_own):
        for order in (5, 4):
            for half in range(2):
                mine = self.place.me == self.owner(order, half)

                @pl.when(self.by_way(order))
                def _():
                    action_way(order, half)

                @pl.when(jnp.logical_not(mine) & jnp.logical_not(self.by_way(order)))
                def _():
                    action_direct(order, half)

                @pl.when(mine)
                def _():
                    action_own(order, half)

    def start(self):
        self.each(
            lambda *at: self.to_way(*at).start(), lambda *at: self.direct(*at).start(), lambda *at: self.own(*at).start()
        )

    def forward(self):
        def action(*at):
            self.pass_in(*at).wait_recv()
            self.pass_on(*at).start()

        self.when_passing(action)

    def finish(self):
        self.each(
            lambda *at: self.to_way(*at).wait_send(),
            lambda *at: self.direct(*at).wait_send(),
            lambda *at: None,
        )
        self.when_passing(lambda *at: self.pass_on(*at).wait_send())
        for order in (5, 4):
            for half in range(2):

                @pl.when(self.place.me == self.owner(order, half))
                def _():
                    pltpu.make_async_copy(self.whole, self.whole, self.sem.at[0]).wait()


def columns(start, size):
    return pl.ds(pl.multiple_of(start, 128), size)


class RowSwap:
    SCRATCH = 2

    @staticmethod
    def scratch():
        return [pltpu.SemaphoreType.DMA((1,)), pltpu.SemaphoreType.DMA((4,))]

    def __init__(self, place, rows_ref, whole_ref, scratch):
        self.place, self.rows_ref, self.whole_ref = place, rows_ref, whole_ref
        self.own_sem, self.sem = scratch
        self.size = rows_ref.shape[0]

    def at(self, core):
        return self.whole_ref.at[pl.ds(pl.multiple_of(core * self.size, self.size), self.size), :]

    def copy(self, slot, source, target, device):
        return pltpu.make_async_remote_copy(
            src_ref=source,
            dst_ref=target,
            send_sem=self.sem.at[slot],
            recv_sem=self.sem.at[slot + 1],
            device_id=device,
            device_id_type=MESH,
        )

    def own(self):
        return pltpu.make_async_copy(self.rows_ref, self.at(self.place.core), self.own_sem.at[0])

    def away(self):
        return self.copy(0, self.rows_ref, self.at(1 - self.place.core), self.place.corner)

    def hand_own(self):
        return self.copy(2, self.rows_ref, self.at(self.place.core), self.place.twin)

    def hand_got(self):
        return self.copy(2, self.at(self.place.core), self.at(self.place.core), self.place.twin)

    def start(self):
        @pl.when(self.place.stays)
        def _():
            self.own().start()
            self.hand_own().start()

        @pl.when(jnp.logical_not(self.place.stays))
        def _():
            self.away().start()

    def step(self):
        @pl.when(jnp.logical_not(self.place.stays))
        def _():
            self.away().wait()
            self.hand_got().start()

    def end(self):
        @pl.when(self.place.stays)
        def _():
            self.own().wait()

        self.hand_got().wait()


class WeightGather:
    def __init__(self, place, line, groups, scratch):
        self.place, self.line, self.groups = place, line, groups
        self.own_sem, self.send_sem, self.recv_sem = scratch
        self.last = len(groups) - 1
        self.to_right, self.to_left = 1, line
        self.half_x, self.half_y, self.rest_y, self.rest_x = (2 * line - 1 + k for k in range(4))

    @staticmethod
    def scratch(count, line):
        dma = pltpu.SemaphoreType.DMA
        return [dma((count,)), dma((count, 2 * line + 3)), dma((count, 2 * line + 3))]

    def copy(self, group, slot, source, target, device):
        return pltpu.make_async_remote_copy(
            src_ref=source,
            dst_ref=target,
            send_sem=self.send_sem.at[group, slot],
            recv_sem=self.recv_sem.at[group, slot],
            device_id=device,
            device_id_type=MESH,
        )

    def same(self, group, slot, region, device):
        return self.copy(group, slot, region, region, device)

    def chunk(self, group, index):
        ref, width, _ = self.groups[group]
        cols = columns(index * width, width)
        if group == self.last:
            return ref.at[:, :, :, :, :, cols]
        return ref.at[:, self.place.y, self.place.x, :, :, cols]

    def corner(self, group, ys, xs, half):
        ref, width, _ = self.groups[group]
        if group == self.last:
            return ref.at[:, ys, xs, half, :, columns(self.place.tensor * width, width)]
        return ref.at[:, ys, xs, half]

    def entry(self, group, half):
        ref, width, _ = self.groups[group]
        return ref.at[:, self.place.y, self.place.x, half, :, columns(self.place.tensor * width, width)]

    def own(self, group):
        core = self.place.core
        return pltpu.make_async_copy(self.groups[group][2](core), self.entry(group, core), self.own_sem.at[group])

    def first(self, group):
        core = self.place.core
        return self.copy(group, 0, self.groups[group][2](1 - core), self.entry(group, core), self.place.twin)

    def begin(self, group):
        self.own(group).start()
        self.first(group).start()

    def enter(self, group):
        self.own(group).wait()
        self.same(group, 0, self.entry(group, 1 - self.place.core), self.place.twin).wait_recv()

    def hop(self, group, step, left):
        t = self.place.tensor
        index = t + step - 1 if left else t - step + 1
        slot = (self.to_left if left else self.to_right) + step - 1
        return self.same(group, slot, self.chunk(group, index), self.place.left if left else self.place.right)

    def arrival(self, group, step, left):
        t = self.place.tensor
        index = t + step if left else t - step
        slot = (self.to_left if left else self.to_right) + step - 1
        return self.same(group, slot, self.chunk(group, index), self.place.right if left else self.place.left)

    def sends(self, step, left):
        t, line = self.place.tensor, self.line
        return (t > 0) & (t + step <= line) if left else (t < line - 1) & (t >= step - 1)

    def line_start(self, group):
        for left in (False, True):

            @pl.when(self.sends(1, left))
            def _():
                self.hop(group, 1, left).start()

    def line_step(self, group, step):
        t, line = self.place.tensor, self.line
        for left in (False, True):

            @pl.when(t + step <= line - 1 if left else t >= step)
            def _():
                self.arrival(group, step, left).wait_recv()

            if step < line - 1:

                @pl.when(self.sends(step + 1, left))
                def _():
                    self.hop(group, step + 1, left).start()

    def line_most(self, group):
        for step in range(1, self.line - 1):
            self.line_step(group, step)

    def line_end(self, group):
        self.line_step(group, self.line - 1)

    def plane_start(self, group):
        place = self.place
        self.same(group, self.half_x, self.corner(group, place.y, place.x, 0), place.across_x).start()
        self.same(group, self.half_y, self.corner(group, place.y, place.x, 1), place.across_y).start()

    def plane_step(self, group):
        place, both = self.place, pl.ds(0, 2)
        self.same(group, self.half_x, self.corner(group, place.y, 1 - place.x, 0), place.across_x).wait_recv()
        self.same(group, self.rest_y, self.corner(group, place.y, both, 0), place.across_y).start()
        self.same(group, self.half_y, self.corner(group, 1 - place.y, place.x, 1), place.across_y).wait_recv()
        self.same(group, self.rest_x, self.corner(group, both, place.x, 1), place.across_x).start()

    def plane_end(self, group):
        place, both = self.place, pl.ds(0, 2)
        self.same(group, self.rest_y, self.corner(group, 1 - place.y, both, 0), place.across_y).wait_recv()
        self.same(group, self.rest_x, self.corner(group, both, 1 - place.x, 1), place.across_x).wait_recv()

    def wait_sends(self, group):
        place, both = self.place, pl.ds(0, 2)
        self.first(group).wait_send()
        for step in range(1, self.line):
            for left in (False, True):

                @pl.when(self.sends(step, left))
                def _():
                    self.hop(group, step, left).wait_send()

        self.same(group, self.half_x, self.corner(group, place.y, place.x, 0), place.across_x).wait_send()
        self.same(group, self.half_y, self.corner(group, place.y, place.x, 1), place.across_y).wait_send()
        self.same(group, self.rest_y, self.corner(group, place.y, both, 0), place.across_y).wait_send()
        self.same(group, self.rest_x, self.corner(group, both, place.x, 1), place.across_x).wait_send()


def add_blocks(target, sources):
    lead, rows = target.shape[:-2], target.shape[-2]
    per = rows // 32

    def body(step, carry):
        block, at = step // per, []
        for size in lead[::-1]:
            at.insert(0, lax.rem(block, size))
            block = block // size
        at = tuple(at) + (pl.ds(pl.multiple_of(lax.rem(step, per) * 32, 32), 32),)
        total = sources[0][at].astype(jnp.float32)
        for source in sources[1:]:
            total = total + source[at].astype(jnp.float32)
        target[at] = total.astype(target.dtype)
        return carry

    lax.fori_loop(0, math.prod(lead) * per, body, 0)


class PlaneSum:
    @staticmethod
    def scratch(count, rows, width):
        pair = pltpu.VMEM((count, 2, rows, width), jnp.bfloat16)
        single = pltpu.VMEM((count, rows, width), jnp.bfloat16)
        dma = pltpu.SemaphoreType.DMA
        return [pair] * 4 + [single] * 2 + [dma((2,)), dma((4,)), dma((4,))]

    SCRATCH = 9

    def __init__(self, place, source, result, scratch):
        self.place, self.source, self.result = place, source, result
        self.own, self.got, self.last = scratch[0:2], scratch[2:4], scratch[4:6]
        self.own_sem, self.send_sem, self.recv_sem = scratch[6:9]

    def copy(self, slot, source, target, device):
        return pltpu.make_async_remote_copy(
            src_ref=source,
            dst_ref=target,
            send_sem=self.send_sem.at[slot],
            recv_sem=self.recv_sem.at[slot],
            device_id=device,
            device_id_type=MESH,
        )

    def cut(self, index, mine):
        both, place = pl.ds(0, 2), self.place
        if index == 0:
            return self.source.at[:, place.y if mine else 1 - place.y, both, 0]
        return self.source.at[:, both, place.x if mine else 1 - place.x, 1]

    def load(self, index):
        return pltpu.make_async_copy(self.cut(index, True), self.own[index], self.own_sem.at[index])

    def first(self, index):
        device = self.place.across_x if index else self.place.across_y
        return self.copy(index, self.cut(index, False), self.got[index], device)

    def second(self, index):
        mine = self.place.y if index else self.place.x
        device = self.place.across_y if index else self.place.across_x
        return self.copy(2 + index, self.own[index].at[:, 1 - mine], self.last[index], device)

    def start(self):
        for index in range(2):
            self.first(index).start()
            self.load(index).start()

    def one(self):
        for index in range(2):
            mine = self.place.y if index else self.place.x
            self.load(index).wait()
            self.first(index).wait_recv()
            own, got = self.own[index], self.got[index]
            add_blocks(own.at[:, 1 - mine], (own.at[:, 1 - mine], got.at[:, 1 - mine]))
            self.second(index).start()
            add_blocks(own.at[:, mine], (own.at[:, mine], got.at[:, mine]))

    def two(self):
        for index in range(2):
            mine = self.place.y if index else self.place.x
            self.second(index).wait_recv()
            add_blocks(self.result.at[:, index], (self.own[index].at[:, mine], self.last[index]))

    def sent(self):
        for index in range(2):
            self.first(index).wait_send()
            self.second(index).wait_send()


class LineSum:
    @staticmethod
    def scratch(shape, line):
        dma = pltpu.SemaphoreType.DMA
        return [pltpu.VMEM(shape, jnp.bfloat16)] * 2 + [dma((2, line)), dma((2, line))]

    SCRATCH = 4

    def __init__(self, place, line, value, result, scratch):
        self.place, self.line, self.value, self.result = place, line, value, result
        self.got = scratch[0:2]
        self.send_sem, self.recv_sem = scratch[2:4]
        self.width = value.shape[-1] // line

    def part(self, ref, index):
        return ref.at[(slice(None),) * (len(ref.shape) - 1) + (slice(index * self.width, (index + 1) * self.width),)]

    def hop(self, index, left):
        return pltpu.make_async_remote_copy(
            src_ref=self.part(self.value, index),
            dst_ref=self.part(self.got[left], index),
            send_sem=self.send_sem.at[left, index],
            recv_sem=self.recv_sem.at[left, index],
            device_id=self.place.left if left else self.place.right,
            device_id_type=MESH,
        )

    def step(self, step):
        for left in range(2):
            for index in range(self.line):
                away = index if left else self.line - 1 - index
                order = step - away
                plane = self.line - 1 - order if left else order
                if order < 0 or (plane <= index if left else plane >= index):
                    continue

                @pl.when(self.place.tensor == plane)
                def _():
                    if order > 0:
                        self.hop(index, left).wait_recv()
                        value = self.part(self.value, index)
                        add_blocks(value, (value, self.part(self.got[left], index)))
                    if away > 0:
                        self.hop(index - 1 if left else index + 1, left).wait_send()
                    self.hop(index, left).start()

    def end(self):
        for index in range(self.line):

            @pl.when(self.place.tensor == index)
            def _():
                sources = [self.part(self.value, index)]
                for left in range(2):
                    if index < self.line - 1 if left else index > 0:
                        self.hop(index, left).wait_recv()
                        sources.append(self.part(self.got[left], index))
                add_blocks(self.result, sources)

    def sent(self):
        for index in range(self.line):

            @pl.when(self.place.tensor == index)
            def _():
                if index > 0:
                    self.hop(index - 1, 1).wait_send()
                if index < self.line - 1:
                    self.hop(index + 1, 0).wait_send()


class HomeCopy:
    def __init__(self, place, value, target, scratch):
        self.place, self.value, self.target = place, value, target
        self.own_sem, self.sem = scratch

    SCRATCH = 2

    @staticmethod
    def scratch():
        return [pltpu.SemaphoreType.DMA((1,)), pltpu.SemaphoreType.DMA((2,))]

    def keep(self):
        return pltpu.make_async_copy(self.value.at[:, self.place.core], self.target, self.own_sem.at[0])

    def give(self):
        return pltpu.make_async_remote_copy(
            src_ref=self.value.at[:, 1 - self.place.core],
            dst_ref=self.target,
            send_sem=self.sem.at[0],
            recv_sem=self.sem.at[1],
            device_id=self.place.twin,
            device_id_type=MESH,
        )

    def start(self):
        self.keep().start()
        self.give().start()

    def wait(self):
        self.keep().wait()
        self.give().wait()


class GroupSum:
    @staticmethod
    def scratch(count, rows, width, line, line_first=False):
        low = jnp.bfloat16
        part = width // line
        done = pltpu.VMEM((count, 2, rows, part), low)
        if line_first:
            whole = (count, 2, 2, 2, rows, width)
            held = [pltpu.VMEM(whole, low), pltpu.VMEM(whole[:-1] + (part,), low), pltpu.SemaphoreType.DMA((1,))]
            plane, along = PlaneSum.scratch(count, rows, part), LineSum.scratch(whole, line)
        else:
            middle = (count, 2, rows, width)
            held = [pltpu.VMEM(middle, low)]
            plane, along = PlaneSum.scratch(count, rows, width), LineSum.scratch(middle, line)
        return held + [done] + plane + along + HomeCopy.scratch()

    def __init__(self, place, line, source, target, scratch, line_first=False):
        scratch = list(scratch)

        def take(count):
            taken = scratch[:count]
            del scratch[:count]
            return taken

        if line_first:
            whole, middle, load_sem = take(3)
            self.load = lambda: pltpu.make_async_copy(source, whole, load_sem.at[0])
        else:
            (middle,) = take(1)
        (done,) = take(1)
        plane, along = take(PlaneSum.SCRATCH), take(LineSum.SCRATCH)
        if line_first:
            self.line = LineSum(place, line, whole, middle, along)
            self.plane = PlaneSum(place, middle, done, plane)
        else:
            self.plane = PlaneSum(place, source, middle, plane)
            self.line = LineSum(place, line, middle, done, along)
        self.home = HomeCopy(place, done, target, take(HomeCopy.SCRATCH))

    def sent(self):
        self.plane.sent()
        self.line.sent()


class VectorSum:
    @staticmethod
    def scratch(shape, line):
        return [
            pltpu.VMEM((4,) + shape, jnp.float32),
            pltpu.VMEM((3,) + shape, jnp.float32),
            pltpu.VMEM((line,) + shape, jnp.float32),
            pltpu.SemaphoreType.DMA((4, max(line, 3))),
        ]

    def __init__(self, place, line, scratch):
        self.place, self.line = place, line
        self.sums, self.got, self.along, self.sem = scratch

    def copy(self, stage):
        place = self.place
        return pltpu.make_async_remote_copy(
            src_ref=self.sums.at[stage],
            dst_ref=self.got.at[stage],
            send_sem=self.sem.at[0, stage],
            recv_sem=self.sem.at[1, stage],
            device_id=(place.twin, place.across_x, place.across_y)[stage],
            device_id_type=MESH,
        )

    def hop(self, other, source):
        return pltpu.make_async_remote_copy(
            src_ref=self.sums.at[3],
            dst_ref=self.along.at[source],
            send_sem=self.sem.at[2, other],
            recv_sem=self.sem.at[3, source],
            device_id=(self.place.dp, other),
            device_id_type=MESH,
        )

    def start(self, value, first_rows):
        self.sums[0] = value
        for index, row in enumerate(first_rows):
            self.sums[0, index : index + 1, :] = row
        self.copy(0).start()

    def step(self, stage):
        self.copy(stage).wait()
        self.sums[stage + 1] = self.sums[stage] + self.got[stage]
        if stage < 2:
            self.copy(stage + 1).start()
            return
        self.along[self.place.tensor] = self.sums[3]
        for other in range(self.line):

            @pl.when(self.place.tensor != other)
            def _():
                self.hop(other, self.place.tensor).start()

    def end(self):
        t = self.place.tensor
        for other in range(self.line):

            @pl.when(t != other)
            def _():
                self.hop(other, t).wait_send()
                self.hop(t, other).wait_recv()

        total = self.along[0]
        for other in range(1, self.line):
            total = total + self.along[other]
        return total


LOG2E = 1.4426950408889634
FAR = 1e32
ROW_BLOCK = 256


def fill_distance(seg_rows, seg_cols, distance):
    def body(step, carry):
        start = pl.multiple_of(step * 64, 64)
        shape = (64, distance.shape[1])
        row = lax.broadcasted_iota(jnp.int32, shape, 0) + start
        col = lax.broadcasted_iota(jnp.int32, shape, 1)
        segs = seg_rows[pl.ds(start, 64), :]
        same = (segs == seg_cols[...]) & (segs > 0) & (col <= row)
        allowed = same | (col == row)
        distance[pl.ds(start, 64), :] = jnp.where(allowed, (row - col).astype(jnp.float32), FAR)
        return carry

    lax.fori_loop(0, distance.shape[0] // 64, body, 0)


def head_lanes(dtype):
    lane = lax.broadcasted_iota(jnp.int32, (1, 2 * HD), 1)
    first = (lane < HD).astype(jnp.float32)
    return (first.astype(dtype), (1.0 - first).astype(dtype))


def attend_group(group, slopes, qkv, mixed, lse, distance):
    length = qkv.shape[1]
    cols = columns(group * 2 * HD, 2 * HD)
    masks = head_lanes(jnp.bfloat16)
    first = head_lanes(jnp.float32)[0] > 0.5
    factor = LOG2E / math.sqrt(HD)
    keys_t = qkv[1, :, cols].T
    values = qkv[2, :, cols]
    for start in range(0, length, ROW_BLOCK):
        stop = start + ROW_BLOCK
        rows = slice(start, stop)
        query = qkv[0, rows, cols]
        parts, sums = [], []
        for head in range(2):
            slope = slopes[2 * group + head] * LOG2E
            scores = jnp.dot(query * masks[head], keys_t[:, :stop], preferred_element_type=jnp.float32)
            scores = scores * factor - slope * distance[rows, :stop]
            top = jnp.max(scores, axis=1, keepdims=True)
            probs = jnp.exp2(scores - top)
            total = jnp.sum(probs, axis=1, keepdims=True)
            out = jnp.dot(probs.astype(jnp.bfloat16), values[:stop], preferred_element_type=jnp.float32)
            parts.append(out / total)
            sums.append(top + jnp.log2(total))
        mixed[rows, cols] = jnp.where(first, parts[0], parts[1]).astype(jnp.bfloat16)
        lse[rows, cols] = jnp.where(first, sums[0], sums[1])


def normalize(rows):
    centred = rows - jnp.mean(rows, axis=1, keepdims=True)
    return centred * lax.rsqrt(jnp.mean(centred * centred, axis=1, keepdims=True) + 1e-05)


def forward_kernel(
    line, attn_ref, mlp_ref, tokens_ref, grads_ref, slopes, seg_rows, seg_cols, qkv_bias, hidden_bias, vectors,
    qkv_w, out_w, up_w, down_w, tokens_out, grads_out, qkv_out, mixed_out, lse_out, normed_out, middle_out,
    hidden_out, act_out, bend_out, *scratch
):
    (x_v, normed, qkv_wv, out_wv, up_wv, qkv, mixed, lse, distance, part, got, middle, hidden, act, bend) = scratch[:15]
    load_sem, store_sem, swap_send, swap_recv = scratch[15:19]
    place = Place()
    narrow, wide = attn_ref.shape[2] // 2, mlp_ref.shape[2] // 4
    size = normed.shape[0]

    def attn_source(index):
        return lambda core: attn_ref.at[index : index + 1, :, columns(core * narrow, narrow)]

    def mlp_source(index, half):
        return lambda core: mlp_ref.at[index : index + 1, :, columns((2 * core + half) * wide, wide)]

    groups = [(qkv_w.at[index : index + 1], narrow, attn_source(index)) for index in range(3)]
    groups.append((out_w, narrow, attn_source(3)))
    groups += [(up_w.at[half : half + 1], wide, mlp_source(0, half)) for half in range(2)]
    groups += [(down_w.at[half : half + 1], wide, mlp_source(1, half)) for half in range(2)]
    query, key, value, outer, up_a, up_b, down_a, down_b = range(8)
    gather = WeightGather(place, line, groups, scratch[19:22])
    tokens = RowSwap(place, tokens_ref, tokens_out, scratch[22:24])
    grads = RowSwap(place, grads_ref, grads_out, scratch[24:26])

    def load(group):
        if group < 3:
            source, target = qkv_w.at[group], qkv_wv.at[group]
        elif group == outer:
            source, target = out_w, out_wv
        else:
            source, target = up_w.at[group - up_a], up_wv.at[group - up_a]
        return pltpu.make_async_copy(source, target, load_sem.at[group])

    x_load = pltpu.make_async_copy(tokens_out, x_v, load_sem.at[7])
    pairs = (
        (qkv, qkv_out),
        (mixed, mixed_out),
        (lse, lse_out),
        (normed, normed_out),
        (middle, middle_out),
        (hidden, hidden_out),
        (act.at[0], act_out.at[0]),
        (act.at[1], act_out.at[1]),
        (bend.at[0], bend_out.at[0]),
        (bend.at[1], bend_out.at[1]),
    )

    def store(index):
        return pltpu.make_async_copy(*pairs[index], store_sem.at[index])

    def normalize_tokens():
        def body(step, carry):
            at = pl.ds(pl.multiple_of(step * 32, 32), 32)
            normal = normalize(x_v[at, :].astype(jnp.float32))
            normed[at, :] = (normal * vectors[0:1, :] + vectors[1:2, :]).astype(jnp.bfloat16)
            return carry

        lax.fori_loop(0, size // 32, body, 0, unroll=4)

    def project(group):
        load(group).wait()
        weight = qkv_wv[group].reshape(size, qkv.shape[2])

        def body(step, carry):
            at = pl.ds(pl.multiple_of(step * 512, 512), 512)
            out = jnp.dot(normed[at, :], weight, preferred_element_type=jnp.float32)
            qkv[group, at, :] = (out + qkv_bias[group : group + 1, :]).astype(jnp.bfloat16)
            return carry

        lax.fori_loop(0, size // 512, body, 0)

    def swap(index):
        at = pl.ds(pl.multiple_of(index * 256, 256), 256)
        return pltpu.make_async_remote_copy(
            src_ref=part.at[at, :],
            dst_ref=got.at[at, :],
            send_sem=swap_send.at[index],
            recv_sem=swap_recv.at[index],
            device_id=place.twin,
            device_id_type=MESH,
        )

    def project_out(index, carry):
        at = pl.ds(pl.multiple_of(index * 256, 256), 256)
        weight = out_wv[0].reshape(size, mixed.shape[1])
        part[at, :] = contract_last(mixed[at, :], weight).astype(jnp.bfloat16)
        swap(index).start()
        return carry

    def add_branch(index, carry):
        swap(index).wait()

        def body(step, carry):
            at = pl.ds(pl.multiple_of(index * 256 + step * 32, 32), 32)
            branch = part[at, :].astype(jnp.float32) + got[at, :].astype(jnp.float32)
            total = x_v[at, :].astype(jnp.float32) + branch + vectors[4:5, :]
            middle[at, :] = total
            hidden[at, :] = (normalize(total) * vectors[5:6, :] + vectors[6:7, :]).astype(jnp.bfloat16)
            return carry

        return lax.fori_loop(0, 8, body, carry, unroll=4)

    def feed(half):
        load(up_a + half).wait()

        def body(step, carry):
            at = pl.ds(pl.multiple_of(step * 256, 256), 256)
            weight = up_wv[half].reshape(size, act.shape[2])
            pre = jnp.dot(hidden[at, :], weight, preferred_element_type=jnp.float32)
            pre = pre + hidden_bias[half : half + 1, :]
            square = pre * pre
            bent = jnp.tanh(0.7978845608 * pre * (1.0 + 0.044715 * square))
            inner = 0.7978845608 * (1.0 + 3.0 * 0.044715 * square)
            act[half, at, :] = (0.5 * pre * (1.0 + bent)).astype(jnp.bfloat16)
            bend[half, at, :] = (0.5 * (1.0 + bent) + 0.5 * pre * (1.0 - bent * bent) * inner).astype(jnp.bfloat16)
            return carry

        lax.fori_loop(0, size // 256, body, 0)
        store(6 + half).start()
        store(8 + half).start()

    greet(place, line)
    for group in (query, down_b, key, value, outer, up_a, up_b, down_a):
        gather.begin(group)
    gather.enter(query)
    gather.line_start(query)
    gather.enter(down_b)
    gather.plane_start(down_b)
    gather.enter(key)
    gather.line_most(query)
    gather.line_start(key)
    tokens.start()
    gather.line_end(query)
    gather.plane_start(query)
    gather.plane_step(down_b)
    gather.enter(value)
    gather.line_most(key)
    gather.line_start(value)
    gather.line_end(key)
    gather.plane_step(query)
    gather.plane_start(key)
    gather.plane_end(down_b)
    gather.line_most(value)
    gather.line_end(value)
    gather.enter(outer)
    gather.line_start(outer)
    gather.plane_end(query)
    load(query).start()
    gather.plane_step(key)
    gather.plane_start(value)
    tokens.step()
    fill_distance(seg_rows, seg_cols, distance)
    gather.enter(up_a)
    gather.line_most(outer)
    gather.line_start(up_a)
    gather.plane_end(key)
    load(key).start()
    gather.line_end(outer)
    gather.plane_step(value)
    gather.plane_start(outer)
    tokens.end()
    x_load.start()
    x_load.wait()
    normalize_tokens()
    store(3).start()
    gather.enter(up_b)
    gather.line_most(up_a)
    gather.line_start(up_b)
    project(query)
    gather.line_end(up_a)
    gather.line_start(down_b)
    gather.plane_end(value)
    load(value).start()
    gather.plane_step(outer)
    gather.plane_start(up_a)
    project(key)
    project(value)
    store(0).start()

    def beside(index):
        if index == 0:
            gather.enter(down_a)
            gather.line_most(up_b)
            gather.line_start(down_a)
            gather.plane_end(outer)
            load(outer).start()
        if index == 1:
            gather.line_end(up_b)
            gather.plane_step(up_a)
            gather.plane_start(up_b)
        if index == 2:
            gather.line_step(down_b, 1)
        if index == 3:
            gather.line_most(down_a)

    def attend(index, carry):
        attend_group(index, slopes, qkv, mixed, lse, distance)
        for order in range(4):

            @pl.when(index == order)
            def _():
                beside(order)

        return carry

    lax.fori_loop(0, qkv.shape[2] // (2 * HD), attend, 0)
    store(1).start()
    store(2).start()
    load(outer).wait()
    lax.fori_loop(0, size // 256, project_out, 0)
    gather.plane_step(up_b)
    gather.line_end(down_a)
    gather.plane_start(down_a)
    lax.fori_loop(0, size // 256, add_branch, 0)
    store(4).start()
    store(5).start()
    for step in range(2, line - 1):
        gather.line_step(down_b, step)
    grads.start()
    gather.plane_end(up_a)
    load(up_a).start()
    feed(0)
    gather.plane_step(down_a)
    gather.plane_end(up_b)
    load(up_b).start()
    feed(1)
    gather.line_end(down_b)
    grads.step()
    gather.plane_end(down_a)
    grads.end()
    for index in range(len(pairs)):
        store(index).wait()
    for group in range(len(groups)):
        gather.wait_sends(group)


def forward(attn_low, mlp_low, tokens, grads, slopes, seg_ids, qkv_bias, hidden_bias, vectors, line):
    rows = attn_low.shape[1]
    narrow, wide = attn_low.shape[2] // 2 * line, mlp_low.shape[2] // 4 * line
    length, width = 2 * tokens.shape[0], tokens.shape[1]
    low, dma = jnp.bfloat16, pltpu.SemaphoreType.DMA
    vmem = pl.BlockSpec(memory_space=pltpu.VMEM)
    hbm = pl.BlockSpec(memory_space=pl.ANY)

    def whole(count, columns_held):
        return (count, 2, 2, 2, rows, columns_held)

    kept = [
        ((3, length, narrow), low),
        ((length, narrow), low),
        ((length, narrow), jnp.float32),
        ((length, width), low),
        ((length, width), jnp.float32),
        ((length, width), low),
        ((2, length, wide), low),
        ((2, length, wide), low),
    ]
    outs = [(whole(3, narrow), low), (whole(1, narrow), low), (whole(2, wide), low), (whole(2, wide), low)]
    outs += [((length, width), low)] * 2 + kept
    held = [(length, width)] * 2 + [whole(3, narrow), whole(1, narrow), whole(2, wide)]
    results = pl.pallas_call(
        functools.partial(forward_kernel, line),
        out_shape=[jax.ShapeDtypeStruct(*each) for each in outs],
        in_specs=[hbm] * 4 + [pl.BlockSpec(memory_space=pltpu.SMEM)] + [vmem] * 5,
        out_specs=[hbm] * len(outs),
        scratch_shapes=[pltpu.VMEM(each, low) for each in held]
        + [pltpu.VMEM(*each) for each in kept[:3]]
        + [pltpu.VMEM((length, length), jnp.float32)]
        + [pltpu.VMEM((length, width), low)] * 2
        + [pltpu.VMEM(*each) for each in kept[4:]]
        + [dma((8,)), dma((10,)), dma((length // 256,)), dma((length // 256,))]
        + WeightGather.scratch(8, line)
        + RowSwap.scratch() * 2,
        compiler_params=pltpu.CompilerParams(
            collective_id=1, has_side_effects=True, vmem_limit_bytes=62 * 1024 * 1024
        ),
        name="forward",
    )(
        attn_low,
        mlp_low,
        tokens,
        grads,
        slopes,
        seg_ids.reshape(-1, 1),
        seg_ids.reshape(1, -1),
        qkv_bias,
        hidden_bias,
        vectors,
    )
    return [each.reshape(each.shape[0], length, -1) for each in results[:4]] + list(results[4:])


def middle_kernel(
    line, grads_ref, act_ref, bend_ref, down_ref, up_ref, hidden_ref, middle_ref, mixed_ref, out_ref, gain,
    down_home, up_out, out_out, mixed_out, mid_out, sums_out, hidden_sums,
    grads, act, pre, down, up, hidden, middle, mixed, weight, part, got, low, mid, down_v, out_v, mixed_v,
    load_sem, store_sem, send_sem, recv_sem, *scratch
):
    place = Place()
    bend, up_v = pre, down
    wide = down_home.shape[2] // 4
    one, two = (
        GroupSum(
            place,
            line,
            down_v.at[half : half + 1],
            down_home.at[:, :, columns((2 * place.core + half) * wide, wide)],
            scratch[half],
        )
        for half in range(2)
    )
    size = grads.shape[0]
    half = size // 2
    blocks = size // 256
    sources = (
        (grads_ref, grads), (down_ref, down), (bend_ref, bend), (up_ref, up), (act_ref.at[0], act.at[0]),
        (middle_ref, middle), (out_ref, weight), (hidden_ref, hidden), (mixed_ref, mixed),
    )
    load_g, load_down, load_bend, load_up, load_act, load_middle, load_out, load_hidden, load_mixed = (
        pltpu.make_async_copy(*each, load_sem.at[index]) for index, each in enumerate(sources)
    )
    load_more = pltpu.make_async_copy(act_ref.at[1], act.at[1], load_sem.at[10])
    for each in (load_g, load_act, load_down, load_bend, load_up, load_more, load_middle, load_out, load_hidden, load_mixed):
        each.start()
    greet(place, line)

    def rows(index, count=256):
        return pl.ds(pl.multiple_of(index * count, count), count)

    def swap(index):
        return pltpu.make_async_remote_copy(
            src_ref=part.at[rows(index), :],
            dst_ref=got.at[rows(index), :],
            send_sem=send_sem.at[index],
            recv_sem=recv_sem.at[index],
            device_id=place.twin,
            device_id_type=MESH,
        )

    def store(slot, index, source, target):
        return pltpu.make_async_copy(source.at[rows(index), :], target.at[rows(index), :], store_sem.at[slot, index])

    def back_hidden(index, carry):
        total = None
        for order in range(2):
            back = jnp.dot(grads[rows(index), :], down[order], preferred_element_type=jnp.float32)
            piece = (back * bend[order, rows(index), :].astype(jnp.float32)).astype(jnp.bfloat16)
            pre[order, rows(index), :] = piece
            column = jnp.sum(piece.astype(jnp.float32), axis=0, keepdims=True)
            hidden_sums[order : order + 1, :] = hidden_sums[order : order + 1, :] + column
            term = contract_last(piece, up[order])
            total = term if total is None else total + term
        part[rows(index), :] = total.astype(jnp.bfloat16)
        swap(index).start()
        return carry

    def down_gradient(order):
        def body(index, carry):
            turned = grads[:, columns(index * 256, 256)].T
            piece = jnp.dot(turned, act[order], preferred_element_type=jnp.float32).astype(jnp.bfloat16)
            down_v[order, index // 2, lax.rem(index, 2)] = piece.reshape(2, 128, piece.shape[1])
            return carry

        lax.fori_loop(0, blocks, body, 0)

    def outer_product(slot, left, rights, targets, outs):
        def body(index, carry):
            turned = left[:, columns(index * 256, 256)].T
            for order, (right, target, out) in enumerate(zip(rights, targets, outs)):
                target[rows(index), :] = jnp.dot(turned, right[...], preferred_element_type=jnp.float32).astype(jnp.bfloat16)
                store(slot + order, index, target, out).start()
            return carry

        lax.fori_loop(0, blocks, body, 0)

    def norm_rows_back(step, sums, owned):
        core = place.core if owned else 1 - place.core
        at = pl.ds(pl.multiple_of(core * half + step * 32, 32), 32)
        grad = part[at, :].astype(jnp.float32) + got[at, :].astype(jnp.float32)
        value = middle[at, :]
        centred = value - jnp.mean(value, axis=1, keepdims=True)
        spread = lax.rsqrt(jnp.mean(centred * centred, axis=1, keepdims=True) + 1e-05)
        hat = centred * spread
        scaled = grad * gain[...]
        inner = jnp.mean(scaled * hat, axis=1, keepdims=True)
        above = grads[at, :].astype(jnp.float32)
        total = above + spread * (scaled - jnp.mean(scaled, axis=1, keepdims=True) - hat * inner)
        low[at, :] = total.astype(jnp.bfloat16)
        if not owned:
            return sums
        mid[pl.ds(pl.multiple_of(step * 32, 32), 32), :] = total
        fold = (4, 8, size)
        terms = (grad * hat, grad, total, above)
        return tuple(one + jnp.sum(term.reshape(fold), axis=0) for one, term in zip(sums, terms))

    def back_mixed(index, carry):
        mixed_v[rows(index), :] = jnp.dot(low[rows(index), :], weight[0], preferred_element_type=jnp.float32).astype(
            jnp.bfloat16
        )
        store(5, index, mixed_v, mixed_out).start()
        return carry

    hidden_sums[...] = jnp.zeros_like(hidden_sums)
    load_g.wait()
    load_act.wait()
    down_gradient(0)
    one.plane.start()
    load_more.wait()
    down_gradient(1)
    two.plane.start()
    load_down.wait()
    load_bend.wait()
    load_up.wait()
    lax.fori_loop(0, blocks // 2, back_hidden, 0)
    one.plane.one()
    lax.fori_loop(blocks // 2, blocks, back_hidden, 0)
    load_middle.wait()
    for index in range(blocks):
        swap(index).wait()
    empty = tuple(jnp.zeros((8, size), jnp.float32) for _ in range(4))
    lax.fori_loop(0, half // 32, lambda step, sums: norm_rows_back(step, sums, False), (), unroll=4)
    two.plane.one()
    one.plane.two()
    one.line.step(0)
    sums = lax.fori_loop(0, half // 32, lambda step, sums: norm_rows_back(step, sums, True), empty, unroll=4)
    for index, each in enumerate(sums):
        sums_out[index : index + 1, :] = jnp.sum(each, axis=0, keepdims=True)
    mid_store = pltpu.make_async_copy(mid, mid_out, load_sem.at[9])
    mid_store.start()
    one.line.step(1)
    load_out.wait()
    lax.fori_loop(0, blocks, back_mixed, 0)
    two.plane.two()
    two.line.step(0)
    load_mixed.wait()
    outer_product(4, low, (mixed,), (out_v.at[0],), (out_out.at[0],))
    for step in range(2, line - 1):
        one.line.step(step)
    two.line.step(1)
    load_hidden.wait()
    outer_product(2, hidden, (pre.at[0], pre.at[1]), (up_v.at[0], up_v.at[1]), (up_out.at[0], up_out.at[1]))
    one.line.end()
    one.home.start()
    for step in range(2, line - 1):
        two.line.step(step)
    two.line.end()
    two.home.start()
    for index in range(blocks):
        for order in range(2):
            store(2 + order, index, up_v.at[order], up_out.at[order]).wait()
        store(4, index, out_v.at[0], out_out.at[0]).wait()
        store(5, index, mixed_v, mixed_out).wait()
    mid_store.wait()
    for group in (one, two):
        group.home.wait()
        group.sent()


def middle_back(grads, act, bend, down, up, hidden, middle, mixed, out, gain, line):
    size, narrow = mixed.shape
    rows = size // 8
    low, dma = jnp.bfloat16, pltpu.SemaphoreType.DMA
    hbm, vmem = pl.BlockSpec(memory_space=pl.ANY), pl.BlockSpec(memory_space=pltpu.VMEM)

    def held(each):
        return pltpu.VMEM(each.shape, each.dtype)

    square = pltpu.VMEM((size, size), low)
    return pl.pallas_call(
        functools.partial(middle_kernel, line),
        out_shape=[
            jax.ShapeDtypeStruct((1, rows, 4 * size // line), low),
            jax.ShapeDtypeStruct(act.shape, low),
            jax.ShapeDtypeStruct((1, size, narrow), low),
            jax.ShapeDtypeStruct((size, narrow), low),
            jax.ShapeDtypeStruct((size // 2, size), jnp.float32),
            jax.ShapeDtypeStruct((4, size), jnp.float32),
            jax.ShapeDtypeStruct((2, size), jnp.float32),
        ],
        in_specs=[hbm] * 9 + [vmem],
        out_specs=[hbm] * 5 + [vmem] * 2,
        scratch_shapes=[held(each) for each in (grads, act, bend, down, up, hidden, middle, mixed, out)]
        + [square, square, square, pltpu.VMEM((size // 2, size), jnp.float32)]
        + [pltpu.VMEM((2, 2, 2, 2, rows, act.shape[2]), low)]
        + [pltpu.VMEM((1, size, narrow), low), pltpu.VMEM((size, narrow), low)]
        + [dma((11,)), dma((6, size // 256)), dma((size // 256,)), dma((size // 256,))]
        + [GroupSum.scratch(1, rows, act.shape[2], line)] * 2,
        compiler_params=pltpu.CompilerParams(
            collective_id=4, has_side_effects=True, vmem_limit_bytes=62 * 1024 * 1024
        ),
        name="middle_back",
    )(grads, act, bend, down, up, hidden, middle, mixed, out, gain.reshape(1, -1))


def attend_back_group(group, slopes, qkv, grad, mixed, lse, out, distance, dk_acc, dv_acc):
    length = qkv.shape[1]
    cols = columns(group * 2 * HD, 2 * HD)
    masks = head_lanes(jnp.bfloat16)
    wide_masks = head_lanes(jnp.float32)
    first = wide_masks[0] > 0.5
    factor = LOG2E / math.sqrt(HD)
    shrink = 1.0 / math.sqrt(HD)
    keys, values = qkv[1, :, cols], qkv[2, :, cols]
    keys_t = keys.T
    values_t = values.T
    dk_acc[...] = jnp.zeros_like(dk_acc)
    dv_acc[...] = jnp.zeros_like(dv_acc)
    for start in range(0, length, ROW_BLOCK):
        stop = start + ROW_BLOCK
        rows = slice(start, stop)
        query, grads, log_sums = qkv[0, rows, cols], grad[rows, cols], lse[rows, cols]
        query_t, grads_t = query.T, grads.T
        product = grads.astype(jnp.float32) * mixed[rows, cols].astype(jnp.float32)
        parts = []
        for head in range(2):
            slope = slopes[2 * group + head] * LOG2E
            lanes = slice(head * HD, (head + 1) * HD)
            scores = jnp.dot(query * masks[head], keys_t[:, :stop], preferred_element_type=jnp.float32)
            log_sum = log_sums[:, head * HD : head * HD + 1]
            probs = jnp.exp2(scores * factor - slope * distance[rows, :stop] - log_sum)
            grad_probs = jnp.dot(grads * masks[head], values_t[:, :stop], preferred_element_type=jnp.float32)
            inner = jnp.sum(product * wide_masks[head], axis=1, keepdims=True)
            grad_scores = (probs * (grad_probs - inner)).astype(jnp.bfloat16)
            parts.append(jnp.dot(grad_scores, keys[:stop], preferred_element_type=jnp.float32))
            dk_acc[lanes, :stop] += jnp.dot(query_t[lanes, :], grad_scores, preferred_element_type=jnp.float32)
            dv_acc[lanes, :stop] += jnp.dot(
                grads_t[lanes, :], probs.astype(jnp.bfloat16), preferred_element_type=jnp.float32
            )
        out[0, rows, cols] = (jnp.where(first, parts[0], parts[1]) * shrink).astype(jnp.bfloat16)
    out[1, :, cols] = (dk_acc[...].T * shrink).astype(jnp.bfloat16)
    out[2, :, cols] = dv_acc[...].T.astype(jnp.bfloat16)


def back_kernel(
    line, up_ref, out_ref, slopes, seg_rows, seg_cols, qkv, grad, mixed, lse, mlp_mom, down_sum, weight_ref, normed_ref,
    act_ref, down_w, attn_home, normed_part, bias_sums, mom_out, whole, out_part,
    held, held_sem, grads, projected, distance, dk_acc, dv_acc, up_sum, mlp_round, *scratch
):
    place = Place()
    narrow_cols = held.shape[2]
    wide, narrow = mlp_mom.shape[2] // 4, attn_home.shape[2] // 2

    def up_target(part):
        return up_sum.at[:, :, columns((2 * place.core + part) * wide, wide)]

    def attn_target(lo, hi):
        return attn_home.at[lo:hi, :, columns(place.core * narrow, narrow)]

    groups = [
        GroupSum(place, line, up_ref.at[0:1], up_target(0), scratch[0]),
        GroupSum(place, line, out_ref, attn_target(3, 4), scratch[1]),
        GroupSum(place, line, projected, attn_target(0, 3), scratch[2]),
        GroupSum(place, line, up_ref.at[1:2], up_target(1), scratch[3], line_first=True),
    ]
    three, outer, inner, last = groups
    collect = Collect(place, mlp_round, whole, scratch[4])

    def attend(group, carry):
        attend_back_group(group, slopes, qkv, grad, mixed, lse, grads, distance, dk_acc, dv_acc)
        return carry

    def halves(ref):
        return [ref.at[:, half * narrow_cols : (half + 1) * narrow_cols] for half in range(2)]

    first_loads = [pltpu.make_async_copy(weight_ref.at[order], held.at[order], held_sem.at[order]) for order in range(3)]
    for half, source in enumerate(halves(normed_ref)):
        first_loads.append(pltpu.make_async_copy(source, held.at[3 + half], held_sem.at[3 + half]))
    quarters = [source for part in range(2) for source in halves(down_w.at[part])]
    late_loads = [pltpu.make_async_copy(quarters[index], held.at[index], held_sem.at[index]) for index in range(4)]

    def act_load(block, index):
        source = act_ref.at[
            index // 2, pl.ds(pl.multiple_of(block * 256, 256), 256), (index % 2) * narrow_cols : (index % 2 + 1) * narrow_cols
        ]
        return pltpu.make_async_copy(source, held.at[4, index * 256 : (index + 1) * 256], held_sem.at[5 + index])

    def project(index, carry):
        left = held[3 + index // 2, :, columns(lax.rem(index, 2) * 256, 256)].T
        for order in range(3):
            piece = jnp.dot(left, grads[order], preferred_element_type=jnp.float32).astype(jnp.bfloat16)
            projected[order, index // 2, lax.rem(index, 2)] = piece.reshape(2, 128, piece.shape[1])
        return carry

    def unproject(index, carry):
        at = pl.ds(pl.multiple_of(index * 256, 256), 256)
        total = contract_last(grads[0, at, :], held[0])
        for order in range(1, 3):
            total = total + contract_last(grads[order, at, :], held[order])
        normed_part[at, :] = total.astype(jnp.bfloat16)
        return carry

    def feed_out(block, carry):
        for index in range(4):
            act_load(block, index).start()
        for index in range(4):
            act_load(block, index).wait()
        total = contract_last(held[4, 0:256], held[0])
        for index in range(1, 4):
            total = total + contract_last(held[4, index * 256 : (index + 1) * 256], held[index])
        at = pl.ds(pl.multiple_of(block * 256, 256), 256)
        for half in range(2):
            grads[half, at, :] = total[:, half * narrow_cols : (half + 1) * narrow_cols].astype(jnp.bfloat16)
        return carry

    def out_store(half):
        return pltpu.make_async_copy(grads.at[half], halves(out_part)[half], held_sem.at[half])

    def update(index, carry):
        at = pl.ds(pl.multiple_of(index * 32, 32), 32)
        for order, gradient in enumerate((up_sum, down_sum)):
            fresh = 0.5 * mlp_mom[order, at, :] + gradient[0, at, :].astype(jnp.float32)
            mom_out[order, at, :] = fresh
            mlp_round[order, at, :] = fresh.astype(jnp.bfloat16)
        return carry

    greet_all(place)
    three.plane.start()
    last.load().start()
    for each in first_loads:
        each.start()
    last.load().wait()
    last.line.step(0)
    outer.plane.start()
    fill_distance(seg_rows, seg_cols, distance)
    pairs = qkv.shape[2] // (2 * HD)
    lax.fori_loop(0, pairs // 2, attend, 0)
    three.plane.one()
    last.line.step(1)
    lax.fori_loop(pairs // 2, pairs, attend, 0)
    three.plane.two()
    three.line.step(0)
    outer.plane.one()
    for each in first_loads:
        each.wait()
    lax.fori_loop(0, 4, project, 0)
    for step in range(2, line - 1):
        last.line.step(step)
    inner.plane.start()
    three.line.step(1)
    outer.plane.two()
    outer.line.step(0)
    lax.fori_loop(0, 4, unproject, 0)
    for each in late_loads:
        each.start()
    for order in range(3):
        bias_sums[order : order + 1, :] = jnp.sum(grads[order].astype(jnp.float32), axis=0, keepdims=True)
    for step in range(2, line - 1):
        three.line.step(step)
    last.line.end()
    last.plane.start()
    three.line.end()
    three.home.start()
    last.plane.one()
    inner.plane.one()
    outer.line.step(1)
    last.plane.two()
    last.home.start()
    for step in range(2, line - 1):
        outer.line.step(step)
    for group in (three, last):
        group.home.wait()
    lax.fori_loop(0, mlp_mom.shape[1] // 32, update, 0)
    collect.start()
    collect.forward()
    outer.line.end()
    outer.home.start()
    inner.plane.two()
    inner.line.step(0)
    for each in late_loads:
        each.wait()
    lax.fori_loop(0, 2, feed_out, 0)
    inner.line.step(1)
    lax.fori_loop(2, 4, feed_out, 0)
    for half in range(2):
        out_store(half).start()
    for step in range(2, line - 1):
        inner.line.step(step)
    inner.line.end()
    inner.home.start()
    inner.home.wait()
    outer.home.wait()
    for half in range(2):
        out_store(half).wait()
    for group in groups:
        group.sent()
    collect.finish()


def attend_back(
    up, out, slopes, seg_ids, qkv, grad, mixed, lse, mlp_mom, down_sum, weights, normed, act, down_w, line
):
    _, length, width = qkv.shape
    rows, wide = up.shape[1] // 8, up.shape[2]
    size = normed.shape[1]
    vmem = pl.BlockSpec(memory_space=pltpu.VMEM)
    hbm = pl.BlockSpec(memory_space=pl.ANY)
    low = jnp.bfloat16
    return pl.pallas_call(
        functools.partial(back_kernel, line),
        out_shape=[
            jax.ShapeDtypeStruct((4, rows, 2 * width // line), low),
            jax.ShapeDtypeStruct((length, size), low),
            jax.ShapeDtypeStruct((3, width), jnp.float32),
            jax.ShapeDtypeStruct(mlp_mom.shape, jnp.float32),
            jax.ShapeDtypeStruct((size, 2 * wide), low),
            jax.ShapeDtypeStruct((length, size), low),
        ],
        in_specs=[hbm] * 2 + [pl.BlockSpec(memory_space=pltpu.SMEM)] + [vmem] * 8 + [hbm] * 4,
        out_specs=[hbm, vmem, vmem, vmem, hbm, hbm],
        scratch_shapes=[
            pltpu.VMEM((5, size, width), low),
            pltpu.SemaphoreType.DMA((9,)),
            pltpu.VMEM(qkv.shape, low),
            pltpu.VMEM((3, 2, 2, 2, rows, width), low),
            pltpu.VMEM((length, length), jnp.float32),
            pltpu.VMEM((2 * HD, length), jnp.float32),
            pltpu.VMEM((2 * HD, length), jnp.float32),
            pltpu.VMEM(down_sum.shape, low),
            pltpu.VMEM(mlp_mom.shape, low),
        ]
        + [GroupSum.scratch(1, rows, wide, line)]
        + [GroupSum.scratch(1, rows, width, line), GroupSum.scratch(3, rows, width, line)]
        + [GroupSum.scratch(1, rows, wide, line, line_first=True), Collect.scratch()],
        compiler_params=pltpu.CompilerParams(
            collective_id=2, has_side_effects=True, vmem_limit_bytes=62 * 1024 * 1024
        ),
        name="attend_back",
    )(
        *(each.reshape(-1, 2, 2, 2, rows, each.shape[2]) for each in (up, out)),
        slopes,
        seg_ids.reshape(-1, 1),
        seg_ids.reshape(1, -1),
        qkv,
        grad,
        mixed,
        lse,
        mlp_mom,
        down_sum,
        weights,
        normed,
        act,
        down_w,
    )


def finish_kernel(
    line, attn_ref, whole_ref, vec_ref, gain, part_ref, x_ref, grad_mid, out_ref, middle_ref, bias, attn_w, mlp_w,
    attn_new, mlp_new, vec_out, dx_new, block_out, *scratch
):
    (thin, full, gram, sent, got, poly, norm_own, norm_got, dx, away, mine) = scratch[:11]
    (home_sem, start_sem, send_sem, back_sem, norm_sem, block_send, block_recv, pass_send, pass_recv, dx_sem) = scratch[11:21]
    vector = VectorSum(Place(), line, scratch[21:25])
    out_mine, out_away, out_sem, middle, tokens, dx_out, attn_home, mlp_home = scratch[25:33]
    place = Place()
    x, y, t, core = place.x, place.y, place.tensor, place.core
    me, devices = place.me, place.devices
    rows = attn_ref.shape[1]
    narrow, wide = attn_ref.shape[2] // 2, mlp_home.shape[2] // 2
    greet_all(place)

    def held(order, index):
        return rows_held(place, thin if order < 4 else full, index, rows, narrow if order < 4 else wide)

    def source(order, half):
        return attn_ref.at[order, :, half * narrow : (half + 1) * narrow]

    def target(order, half):
        if order < 4:
            return attn_home.at[order, :, half * narrow : (half + 1) * narrow]
        return mlp_home.at[order - 4, :, half * wide : (half + 1) * wide]

    def owner_of(order, half):
        ox, oy, oz = OWNERS[order]
        return place.index(ox, oy, half, oz)

    def owns(order):
        ox, oy, oz = OWNERS[order]
        return (x == ox) & (y == oy) & (t == oz)

    owns_full = owns(4) | owns(5)
    owns_thin = owns(0) | owns(1) | owns(2) | owns(3)

    def collect(order, half):
        return remote(
            place, source(order, half), held(order, me), home_sem.at[order, half], start_sem.at[0], owner_of(order, half)
        )

    def collect_own(order, half):
        return pltpu.make_async_copy(source(order, half), held(order, me), start_sem.at[0])

    @pl.when(owns_full)
    def _():
        pltpu.make_async_copy(whole_ref, full, start_sem.at[0]).start()

    for order in range(4):
        for half in range(2):

            @pl.when(me == owner_of(order, half))
            def _():
                collect_own(order, half).start()

            @pl.when(me != owner_of(order, half))
            def _():
                collect(order, half).start()

    half_rows = dx.shape[0]

    def rows_of(ref, cores):
        return ref.at[pl.ds(pl.multiple_of(cores * half_rows, half_rows), half_rows), :]

    part_swap = pltpu.make_async_remote_copy(
        src_ref=rows_of(part_ref, 1 - core),
        dst_ref=away,
        send_sem=dx_sem.at[0],
        recv_sem=dx_sem.at[1],
        device_id=place.twin,
        device_id_type=MESH,
    )
    part_load = pltpu.make_async_copy(rows_of(part_ref, core), mine, dx_sem.at[2])
    part_swap.start()
    part_load.start()
    out_load = pltpu.make_async_copy(rows_of(out_ref, core), out_mine, out_sem.at[0])
    out_swap = pltpu.make_async_remote_copy(
        src_ref=rows_of(out_ref, 1 - core),
        dst_ref=out_away,
        send_sem=out_sem.at[3],
        recv_sem=out_sem.at[4],
        device_id=place.twin,
        device_id_type=MESH,
    )
    middle_load = pltpu.make_async_copy(rows_of(middle_ref, core), middle, out_sem.at[1])
    tokens_load = pltpu.make_async_copy(rows_of(x_ref, core), tokens, out_sem.at[2])
    for each in (tokens_load, out_load, out_swap, middle_load):
        each.start()

    def out_rows(step, carry):
        at = pl.ds(pl.multiple_of(step * 32, 32), 32)
        total = out_mine[at, :].astype(jnp.float32) + out_away[at, :].astype(jnp.float32)
        out_mine[at, :] = (middle[at, :] + total + bias[...]).astype(jnp.bfloat16)
        return carry

    def go_home(slot, source_ref, target_ref, sem):
        keep_rows = pltpu.make_async_copy(source_ref, target_ref, sem.at[slot])
        move_rows = pltpu.make_async_remote_copy(
            src_ref=source_ref,
            dst_ref=target_ref,
            send_sem=sem.at[slot + 1],
            recv_sem=sem.at[slot + 2],
            device_id=place.corner,
            device_id_type=MESH,
        )
        return keep_rows, move_rows

    dx_moves = go_home(2, dx, dx_out, dx_sem)
    out_moves = go_home(5, out_mine, block_out, out_sem)

    def when_moving(moves, action):
        for moving in (False, True):

            @pl.when(place.stays != moving)
            def _():
                action(moves[moving])

    step_rows = 32

    def dx_rows(step, sums):
        at = pl.ds(pl.multiple_of(step * step_rows, step_rows), step_rows)
        grad = mine[at, :].astype(jnp.float32) + away[at, :].astype(jnp.float32)
        value = tokens[at, :].astype(jnp.float32)
        centred = value - jnp.mean(value, axis=1, keepdims=True)
        spread = lax.rsqrt(jnp.mean(centred * centred, axis=1, keepdims=True) + 1e-05)
        hat = centred * spread
        product = grad * hat
        scaled = grad * gain[...]
        inner = jnp.mean(scaled * hat, axis=1, keepdims=True)
        back_grad = spread * (scaled - jnp.mean(scaled, axis=1, keepdims=True) - hat * inner)
        dx[at, :] = (grad_mid[at, :] + back_grad).astype(jnp.bfloat16)
        fold = (step_rows // 8, 8, grad.shape[1])
        return (
            sums[0] + jnp.sum(product.reshape(fold), axis=0),
            sums[1] + jnp.sum(grad.reshape(fold), axis=0),
        )

    part_swap.wait()
    part_load.wait()
    tokens_load.wait()
    empty = jnp.zeros((8, gain.shape[1]), jnp.float32)
    token_sums = lax.fori_loop(0, half_rows // step_rows, dx_rows, (empty, empty), unroll=2)
    when_moving(dx_moves, lambda move: move.start())
    vector.start(vec_ref[...], [jnp.sum(each, axis=0, keepdims=True) for each in token_sums])
    out_load.wait()
    out_swap.wait()
    middle_load.wait()
    lax.fori_loop(0, half_rows // 32, out_rows, 0, unroll=2)
    when_moving(out_moves, lambda move: move.start())

    def contract_rows(left, right):
        return lax.dot_general(left, right, (((1,), (1,)), ((), ())), preferred_element_type=jnp.float32)

    block = 256

    def swap_block(slot, index):
        return pltpu.make_async_remote_copy(
            src_ref=sent.at[index],
            dst_ref=got.at[slot, index],
            send_sem=block_send.at[index],
            recv_sem=block_recv.at[slot, index],
            device_id=place.twin,
            device_id_type=MESH,
        )

    def begin(matrix):
        size, width = matrix.shape
        pltpu.make_async_copy(matrix, matrix, start_sem.at[0]).wait()

        def add_squares(step, total):
            piece = matrix[pl.ds(pl.multiple_of(step * 32, 32), 32), :].astype(jnp.float32)
            piece = piece * piece
            return total + jnp.sum(piece.reshape(4, 8, width // 128, 128), axis=(0, 2))

        squares = lax.fori_loop(0, size // 32, add_squares, jnp.zeros((8, 128), jnp.float32))
        norm_own[...] = jnp.zeros((8, 128), jnp.float32) + jnp.sum(squares)
        swap = pltpu.make_async_remote_copy(
            src_ref=norm_own,
            dst_ref=norm_got,
            send_sem=norm_sem.at[0],
            recv_sem=norm_sem.at[1],
            device_id=place.twin,
            device_id_type=MESH,
        )
        swap.start()
        swap.wait()
        scale = 1.0 / (jnp.sqrt(norm_own[...] + norm_got[...]) + 1e-06)
        scale = scale[0:1, 0:1]

        def scale_rows(step, carry):
            at = pl.ds(pl.multiple_of(step * 32, 32), 32)
            matrix[at, :] = (matrix[at, :].astype(jnp.float32) * scale).astype(jnp.bfloat16)
            return carry

        lax.fori_loop(0, size // 32, scale_rows, 0)

    def iterate(matrix, repeat):
        size, width = matrix.shape
        blocks = size // block
        slot = repeat % 2

        def share(index, carry):
            at = pl.ds(pl.multiple_of(index * block, block), block)
            sent[index] = contract_rows(matrix[at, :], matrix[...]).astype(jnp.bfloat16)
            swap_block(slot, index).start()
            return carry

        lax.fori_loop(0, blocks, share, 0)

        def add(index, carry):
            at = pl.ds(pl.multiple_of(index * block, block), block)
            swap_block(slot, index).wait()
            total = sent[index].astype(jnp.float32) + got[slot, index].astype(jnp.float32)
            gram[at, :] = total.astype(jnp.bfloat16)
            return carry

        lax.fori_loop(0, blocks, add, 0)
        square = jnp.dot(gram[...], gram[...], preferred_element_type=jnp.float32)
        poly[...] = (coeff_b * gram[...].astype(jnp.float32) + coeff_c * square).astype(jnp.bfloat16)
        step_width = min(width, 1024)

        def advance(index, carry):
            at = columns(index * step_width, step_width)
            moved = jnp.dot(poly[...], matrix[:, at], preferred_element_type=jnp.float32)
            matrix[:, at] = (coeff_a * matrix[:, at].astype(jnp.float32) + moved).astype(jnp.bfloat16)
            return carry

        lax.fori_loop(0, width // step_width, advance, 0)

    @pl.when(owns_thin)
    def _():
        begin(thin)

    @pl.when(owns_full)
    def _():
        begin(full)

    for repeat in range(NS_STEPS):

        @pl.when(owns_thin)
        def _():
            iterate(thin, repeat)

        @pl.when(owns_full)
        def _():
            iterate(full, repeat)

        if repeat < 3:
            vector.step(repeat)
        if repeat == 3:
            vec_out[...] = vector.end()

    def keep(order, half):
        return pltpu.make_async_copy(held(order, me), target(order, half), back_sem.at[order, half])

    def back(order, half, index):
        return remote(place, held(order, index), target(order, half), send_sem.at[0], back_sem.at[order, half], index)

    def place_in(index):
        dp, z = place.of(index)
        return lax.rem(dp // 2, 2), dp // 4, z, lax.rem(dp, 2)

    def one_aside(order, xs, ys):
        ox, oy, _ = OWNERS[order]
        return (xs != ox) != (ys != oy)

    def back_by_way(order, index):
        xs, ys, z, _ = place_in(index)
        return one_aside(order, xs, ys) & is_one_of(z, sides(order, line)[0])

    def to_back_way(order, half, index):
        xs, ys, z, cores = place_in(index)
        region = held(order, index)
        first = sides(order, line)[0][0]
        return remote(
            place, region, region, send_sem.at[0], pass_recv.at[z - first, cores], place.index(xs, ys, half, OWNERS[order][2])
        )

    def back_in(order, which, cores):
        index = place.index(x, y, cores, sides(order, line)[0][which])
        region = held(order, index)
        return remote(place, region, region, pass_send.at[which, cores], pass_recv.at[which, cores], index)

    def back_on(order, half, which, cores):
        index = place.index(x, y, cores, sides(order, line)[0][which])
        return remote(
            place, held(order, index), target(order, half), pass_send.at[which, cores], back_sem.at[order, half], index
        )

    def when_back_way(order, action):
        for half in range(2):

            @pl.when(one_aside(order, x, y) & (t == OWNERS[order][2]) & (core == half))
            def _():
                for which in range(len(sides(order, line)[0])):
                    for cores in range(2):
                        action(order, half, which, cores)

    def each_device(order, half, action, passed):
        def body(step, carry):
            index = lax.rem(me + step, devices)
            if order < 4:
                action(order, half, index)
            else:

                @pl.when(back_by_way(order, index) == passed)
                def _():
                    action(order, half, index)

            return carry

        lax.fori_loop(1, devices, body, 0)

    def give_back(orders):
        for order in orders:
            for half in range(2):

                @pl.when(me == owner_of(order, half))
                def _():
                    if order >= 4:
                        each_device(order, half, lambda *at: to_back_way(*at).start(), True)
                    each_device(order, half, lambda *at: back(*at).start(), False)
                    keep(order, half).start()

    give_back((4, 5, 0, 1, 2, 3))

    def return_rows(order, half, which, cores):
        back_in(order, which, cores).wait_recv()
        back_on(order, half, which, cores).start()

    for order in (4, 5):
        when_back_way(order, return_rows)

    for order in range(6):
        for half in range(2):
            keep(order, half).wait()

            @pl.when(me == owner_of(order, half))
            def _():
                if order >= 4:
                    each_device(order, half, lambda *at: to_back_way(*at).wait_send(), True)
                each_device(order, half, lambda *at: back(*at).wait_send(), False)

            if order < 4:

                @pl.when(me != owner_of(order, half))
                def _():
                    collect(order, half).wait_send()

    for order in (4, 5):
        when_back_way(order, lambda *at: back_on(*at).wait_send())

    when_moving(dx_moves, lambda move: move.wait())

    def widen(step, carry):
        at = pl.ds(pl.multiple_of(step * 32, 32), 32)
        dx_new[at, :] = dx_out[at, :].astype(jnp.float32)
        return carry

    lax.fori_loop(0, half_rows // 32, widen, 0)

    def renew(step, carry):
        at = pl.ds(pl.multiple_of(step * 32, 32), 32)
        for order in range(4):
            attn_new[order, at, :] = attn_w[order, at, :] - attn_home[order, at, :].astype(jnp.float32)
        for order in range(2):
            change = math.sqrt(FF / D) * mlp_home[order, at, :].astype(jnp.float32)
            mlp_new[order, at, :] = mlp_w[order, at, :] - change
        return carry

    lax.fori_loop(0, rows // 32, renew, 0)
    when_moving(out_moves, lambda move: move.wait())


def finish(attn_round, mlp_whole, vec, gain, normed_part, tokens, grad_mid, out_part, middle, bias, attn_w, mlp_w, line):
    rows = attn_w.shape[1]
    size = 8 * rows
    narrow, wide = attn_w.shape[2] // 2 * line, mlp_w.shape[2] // 2 * line
    low, dma = jnp.bfloat16, pltpu.SemaphoreType.DMA
    hbm = pl.BlockSpec(memory_space=pl.ANY)
    vmem = pl.BlockSpec(memory_space=pltpu.VMEM)
    half = grad_mid.shape
    return pl.pallas_call(
        functools.partial(finish_kernel, line),
        out_shape=[
            jax.ShapeDtypeStruct(attn_w.shape, jnp.float32),
            jax.ShapeDtypeStruct(mlp_w.shape, jnp.float32),
            jax.ShapeDtypeStruct(vec.shape, jnp.float32),
            jax.ShapeDtypeStruct(half, jnp.float32),
            jax.ShapeDtypeStruct(half, low),
        ],
        in_specs=[hbm, hbm, vmem, vmem, hbm, hbm, vmem, hbm, hbm, vmem, vmem, vmem],
        out_specs=[vmem, vmem, vmem, vmem, hbm],
        scratch_shapes=[
            pltpu.VMEM((size, narrow), low),
            pltpu.VMEM((size, wide), low),
            pltpu.VMEM((size, size), low),
            pltpu.VMEM((size // 256, 256, size), low),
            pltpu.VMEM((2, size // 256, 256, size), low),
            pltpu.VMEM((size, size), low),
            pltpu.VMEM((8, 128), jnp.float32),
            pltpu.VMEM((8, 128), jnp.float32),
            pltpu.VMEM(half, low),
            pltpu.VMEM(half, low),
            pltpu.VMEM(half, low),
            dma((6, 2)),
            dma((1,)),
            dma((1,)),
            dma((6, 2)),
            dma((2,)),
            dma((size // 256,)),
            dma((2, size // 256)),
            dma((2, 2)),
            dma((2, 2)),
            dma((5,)),
        ]
        + VectorSum.scratch(vec.shape, line)
        + [
            pltpu.VMEM(half, low),
            pltpu.VMEM(half, low),
            dma((8,)),
            pltpu.VMEM(half, jnp.float32),
            pltpu.VMEM(half, low),
            pltpu.VMEM(half, low),
            pltpu.VMEM(attn_w.shape, low),
            pltpu.VMEM(mlp_w.shape, low),
        ],
        compiler_params=pltpu.CompilerParams(
            collective_id=3, has_side_effects=True, vmem_limit_bytes=60 * 1024 * 1024
        ),
        name="finish",
    )(
        attn_round,
        mlp_whole,
        vec,
        gain.reshape(1, -1),
        normed_part,
        tokens,
        grad_mid,
        out_part,
        middle,
        bias.reshape(1, -1),
        attn_w,
        mlp_w,
    )


def pair_swap(value):
    dp, line = lax.axis_size("dp"), lax.axis_size("tensor")
    pairs = [(i * line + k, (i ^ 1) * line + k) for i in range(dp) for k in range(line)]
    return lax.ppermute(value, ("dp", "tensor"), pairs)


def on_chip_pair(tokens, cotangent, segments, attn_w, mlp_w, vectors, attn_mom, mlp_mom, vector_mom):
    line = lax.axis_size("tensor")
    place = Place()
    core, t = place.core, place.tensor
    width = tokens.shape[1]
    narrow, wide = attn_w.shape[2] // 2, mlp_w.shape[2] // 4
    total_tokens = tokens.shape[0] * line * lax.axis_size("dp")

    def my_columns(row):
        return lax.dynamic_index_in_dim(row.reshape(line, 2, narrow), core, 1, False).reshape(-1)

    def place_columns(piece):
        spread = jnp.zeros((line, 2, narrow), jnp.float32)
        return lax.dynamic_update_slice(spread, piece.reshape(line, 1, narrow), (0, core, 0)).reshape(-1)

    hidden_bias = lax.dynamic_index_in_dim(vectors[8:].reshape(line, 2, 2, wide), core, 1, False)
    hidden_bias = hidden_bias.transpose(1, 0, 2).reshape(2, line * wide)

    seg_pairs = segments.reshape(-1, SEQ)
    seg_own = lax.dynamic_index_in_dim(seg_pairs, t // 2, 0, False)
    seg_ids = jnp.where(core == lax.rem(t, 2), seg_own, pair_swap(seg_own))

    biases = jnp.stack([my_columns(vectors[2]), jnp.zeros((narrow * line,), jnp.float32), my_columns(vectors[3])])
    per = narrow // HD
    local_ids = jnp.arange(per * line)
    head_ids = (local_ids // per) * (2 * per) + core * per + local_ids % per
    slopes = jnp.exp2(-(8.0 / HEADS) * (head_ids.astype(jnp.float32) + 1.0))
    low = jnp.bfloat16
    (
        wqkv, wout, w_up, w_down, x_low, grad_low, qkv, mixed, log_sums, normed, middle, hidden_low, hidden_act, bend
    ) = forward(
        attn_w.astype(low),
        mlp_w.astype(low),
        tokens,
        cotangent,
        slopes,
        seg_ids,
        biases,
        hidden_bias,
        vectors,
        line,
    )
    down_sum, grad_up, grad_out, grad_mixed, grad_mid_mine, middle_sums, hidden_sums = middle_back(
        grad_low, hidden_act, bend, w_down, w_up, hidden_low, middle, mixed, wout, vectors[5], line
    )
    attn_sum, normed_part, bias_sums, mlp_mom_new, mlp_whole, out_part = attend_back(
        grad_up,
        grad_out,
        slopes,
        seg_ids,
        qkv,
        grad_mixed,
        mixed,
        log_sums,
        mlp_mom,
        down_sum,
        wqkv,
        normed,
        hidden_act,
        w_down,
        line,
    )
    hidden_grad = lax.dynamic_update_slice(
        jnp.zeros((line, 2, 2, wide), jnp.float32),
        hidden_sums.reshape(2, line, wide).transpose(1, 0, 2)[:, None],
        (0, core, 0, 0),
    )
    vector_rows = jnp.stack(
        [
            jnp.zeros((width,), jnp.float32),
            jnp.zeros((width,), jnp.float32),
            place_columns(bias_sums[0]),
            place_columns(bias_sums[2]),
            middle_sums[2],
            middle_sums[0],
            middle_sums[1],
            middle_sums[3],
        ]
    )
    vector_local = jnp.concatenate([vector_rows, hidden_grad.reshape(-1, width)], axis=0)
    padding = jnp.zeros((4, width), jnp.float32)
    attn_mom_new = 0.5 * attn_mom + attn_sum.astype(jnp.float32)
    attn_new, mlp_new, vector_sum, grad_tokens, output = finish(
        attn_mom_new.astype(low),
        mlp_whole,
        jnp.concatenate([vector_local, padding], axis=0),
        vectors[0],
        normed_part,
        x_low,
        grad_mid_mine,
        out_part,
        middle,
        vectors[7],
        attn_w,
        mlp_w,
        line,
    )
    vector_grads = vector_sum[: vector_local.shape[0]]
    vector_mom_new = 0.5 * vector_mom + vector_grads
    vector_new = vectors - 0.1 / math.sqrt(total_tokens) * vector_mom_new
    return (
        output,
        grad_tokens,
        attn_mom_new,
        attn_new,
        mlp_mom_new,
        mlp_new,
        vector_mom_new,
        vector_new,
    )


def solution(mesh):
    in_specs = (
        P(("dp", "tensor"), None),
        P(("dp", "tensor"), None),
        P("dp"),
        P(None, "dp", "tensor"),
        P(None, "dp", "tensor"),
        P(),
        P(None, "dp", "tensor"),
        P(None, "dp", "tensor"),
        P(),
    )
    out_specs = (
        P(("dp", "tensor"), None),
        P(("dp", "tensor"), None),
        P(None, "dp", "tensor"),
        P(None, "dp", "tensor"),
        P(None, "dp", "tensor"),
        P(None, "dp", "tensor"),
        P(),
        P(),
    )
    chips_of_two = (mesh.shape["dp"], mesh.shape["tensor"]) == (8, 4)
    return jax.shard_map(
        on_chip_pair if chips_of_two else on_device, mesh=mesh, in_specs=in_specs, out_specs=out_specs, check_vma=False
    )
```

profile of v0, /device:TPU:0, one launch (start us, length us, event | category | flops | bytes accessed | tf_op | source)
XLA Modules:
  0.0 453.8 jit_solution(13705226185979635706)
XLA Ops:
  0.7 0.8 reshape.59
  2.0 1.5 fusion.8
  3.5 0.8 slice.40
  4.4 0.7 pad_maximum_fusion.qkv_bias
  5.1 0.6 fusion.4.slopes
  5.6 0.6 copy.33
  6.2 2.1 convert_element_type.16.mlp_ref
  8.3 0.7 convert_element_type.15.attn_ref
  9.1 1.0 copy.26.seg_rows
  10.1 141.6 %forward.1 = (bf16[3,2,2,2,128,512]{5,4,3,2,1,0:T(8,128)(2,1)}, bf16[1,2,2,2,128,512]{5,4,3,2,1,0:T(8,128)(2,1)}, bf16[2,2,2,2,128,1024]{5,4,3,2,1,0:T(8,128)(2,...) custom-call(bf16[4,128,256]{2,1,0:T(8,128)(2,1)} %convert_element_ty, ...), custom_call_target="tpu_custom_call" | custom-call | tf_op jit(solution)/shard_map/forward/pallas_call | solution.py:1431
  151.7 61.4 %middle_back.1 = (bf16[1,128,1024]{2,1,0:T(8,128)(2,1)}, bf16[2,1024,1024]{2,1,0:T(8,128)(2,1)}, bf16[1,1024,512]{2,1,0:T(8,128)(2,1)}, bf16[1024,512]{1,0:T(8,1...) custom-call(bf16[1024,1024]{1,0:T(8,128)(2,1)} %get-tuple-element.40.grads_ref, ...), custom_call_target="tpu_custom_call" | custom-call | tf_op jit(solution)/shard_map/middle_back/pallas_call | solution.py:1639
  213.1 0.8 fusion.9
  213.9 0.7 slice.45
  214.7 111.7 %attend_back.1 = (bf16[4,128,256]{2,1,0:T(8,128)(2,1)}, bf16[1024,1024]{1,0:T(8,128)(2,1)}, f32[3,512]{1,0:T(4,128)}, f32[2,128,1024]{2,1,0:T(8,128)}, bf16[1024...) custom-call(bf16[2,2,2,2,128,1024]{5,4,3,2,1,0:T(8,128)(2,1)} %bitcast.44, bf16[1,2,2,2,128,512]{5,4,3,2,1,0:T(8,128)(2,1)} %bitcast.48, ...), custom_call_target="tpu_custom_call" | custom-call | tf_op jit(solution)/shard_map/attend_back/pallas_call | solution.py:1868
  326.3 0.8 slice_bitcast_fusion
  327.3 1.9 fusion.7
  329.2 1.3 concatenate.3.vec_ref
  330.5 114.9 %finish.1 = (f32[4,128,256]{2,1,0:T(8,128)}, f32[2,128,1024]{2,1,0:T(8,128)}, f32[16,1024]{1,0:T(8,128)}, f32[512,1024]{1,0:T(8,128)}, bf16[512,1024]{1,0:T(8,128)(2,1)}) custom-call(bf16[4,128,256]{2,1,0:T(8,128)(2,1)} %get-tuple-element.74.attn_ref, bf16[1024,2048]{1,0:T(8,128)(2,1)} %get-tuple-element.58.whole_ref, f32[16,1024]{1,0:T(8,128)} %concatenate.3.vec_ref, ...), custom_call_target="tpu_custom_call" | custom-call | tf_op jit(solution)/shard_map/finish/pallas_call | solution.py:2299
  445.4 1.6 multiply_subtract_fusion
  447.0 2.3 copy.45
  449.3 1.3 copy.46
  450.7 0.8 copy.47
  451.5 1.0 copy.48
  452.4 1.0 copy.49
  (38 shorter events, 0.9 us)
Async XLA Ops:
  0.6 7.7 %copy-start = (f32[4,128,256]{2,1,0:T(8,128)S(1)}, f32[4,128,256]{2,1,0:T(8,128)}, u32[]{:S(2)}) copy-start(f32[4,128,256]{2,1,0:T(8,128)} %attn_w.1) | copy-start | bytes 1572868
  1.4 7.6 %collective-permute-start = (s32[1024]{0:T(1024)S(1)}, s32[1024]{0:T(1024)S(1)}, u32[]{:S(2)}, u32[]{:S(2)}) collective-permute-start(s32[1024]{0:T(1024)S(1)} %bitcast.54), channel_id=1, source_target_pairs={{0,4},{1,5},{2,6},{3,7},{4,0},{5,1},{6,2},{7,3},{8,12},{9,13},{10,... | collective-permute-start | bytes 12296 | tf_op jit(solution)/shard_map/ppermute | solution.py:2367
  9.1 1.0 copy-start.8
  214.7 112.5 %copy-start.9 = (f32[2,1024]{1,0:T(2,128)S(1)}, f32[2,1024]{1,0:T(2,128)}, u32[]{:S(2)}) copy-start(f32[2,1024]{1,0:T(2,128)} %get-tuple-element.61) | copy-start | bytes 24580
  214.7 112.6 %copy-start.4 = (f32[4,128,256]{2,1,0:T(8,128)S(1)}, f32[4,128,256]{2,1,0:T(8,128)}, u32[]{:S(2)}) copy-start(f32[4,128,256]{2,1,0:T(8,128)} %param.15) | copy-start | bytes 1572868
  330.5 114.9 %copy-start.6 = (f32[12,1024]{1,0:T(8,128)S(1)}, f32[12,1024]{1,0:T(8,128)}, u32[]{:S(2)}) copy-start(f32[12,1024]{1,0:T(8,128)} %vectors.1) | copy-start | bytes 147460
  330.5 114.9 %copy-start.7 = (f32[12,1024]{1,0:T(8,128)S(1)}, f32[12,1024]{1,0:T(8,128)}, u32[]{:S(2)}) copy-start(f32[12,1024]{1,0:T(8,128)} %param.17) | copy-start | bytes 147460
  445.3 3.9 copy-start.1
  449.3 1.4 copy-start.5
  449.3 2.2 copy-start.2
  450.7 1.8 copy-start.3
where the time goes:
time: 462 us; the launch traced here: 454 us
  Pallas kernels  430 us (93%)
  local copies, waits for them, and re-layouts  15 us (3%)
  other arithmetic  7.6 us (2%)
    pallas_call x1, Pallas kernels, forward(): pl.pallas_call(functools.partial(forward_kernel, line), out_shape=[jax.Sh...  142 us
    pallas_call x1, Pallas kernels, finish(): pl.pallas_call(functools.partial(finish_kernel, line), out_shape=[jax.Sha...  115 us
    pallas_call x1, Pallas kernels, attend_back(): pl.pallas_call(functools.partial(back_kernel, line), out_shape=[jax.Shape...  112 us
    pallas_call x1, Pallas kernels, middle_back(): pl.pallas_call(functools.partial(middle_kernel, line), out_shape=[jax.Sha...  61.4 us
  transfers between devices with their start and end apart: 1, of which 0 were waited for; matrix products, arithmetic and copies ran while one was open for 2% of the time, Pallas kernels for 0%

commit v1 on v0

--- a/solution.py
+++ b/solution.py
@@ -608,11 +608,11 @@
 
 
 class RowSwap:
-    SCRATCH = 2
+    PARTS = 4
 
     @staticmethod
     def scratch():
-        return [pltpu.SemaphoreType.DMA((1,)), pltpu.SemaphoreType.DMA((4,))]
+        return [pltpu.SemaphoreType.DMA((1,)), pltpu.SemaphoreType.DMA((2 + 2 * RowSwap.PARTS,))]
 
     def __init__(self, place, rows_ref, whole_ref, scratch):
         self.place, self.rows_ref, self.whole_ref = place, rows_ref, whole_ref
@@ -635,37 +635,91 @@
     def own(self):
         return pltpu.make_async_copy(self.rows_ref, self.at(self.place.core), self.own_sem.at[0])
 
-    def away(self):
-        return self.copy(0, self.rows_ref, self.at(1 - self.place.core), self.place.corner)
+    def away(self, part):
+        count = self.size // self.PARTS
+        start = pl.multiple_of((1 - self.place.core) * self.size + part * count, count)
+        source = self.rows_ref.at[part * count : (part + 1) * count, :]
+        return self.copy(2 + 2 * part, source, self.whole_ref.at[pl.ds(start, count), :], self.place.corner)
 
     def hand_own(self):
-        return self.copy(2, self.rows_ref, self.at(self.place.core), self.place.twin)
+        return self.copy(0, self.rows_ref, self.at(self.place.core), self.place.twin)
 
     def hand_got(self):
-        return self.copy(2, self.at(self.place.core), self.at(self.place.core), self.place.twin)
+        return self.copy(0, self.at(self.place.core), self.at(self.place.core), self.place.twin)
+
+    def start(self, parts):
+        if 0 in parts:
+
+            @pl.when(self.place.stays)
+            def _():
+                self.own().start()
+                self.hand_own().start()
+
+        @pl.when(jnp.logical_not(self.place.stays))
+        def _():
+            for part in parts:
+                self.away(part).start()
+
+    def step(self):
+        @pl.when(jnp.logical_not(self.place.stays))
+        def _():
+            for part in range(self.PARTS):
+                self.away(part).wait()
+            self.hand_got().start()
+
+    def end(self):
+        @pl.when(self.place.stays)
+        def _():
+            self.own().wait()
+
+        self.hand_got().wait()
+
+
+class CornerMove:
+    PARTS = 4
+
+    @staticmethod
+    def scratch():
+        return [pltpu.SemaphoreType.DMA((1,)), pltpu.SemaphoreType.DMA((2, CornerMove.PARTS))]
+
+    def __init__(self, place, rows_ref, target_ref, scratch):
+        self.place, self.rows_ref, self.target_ref = place, rows_ref, target_ref
+        self.own_sem, self.sem = scratch
+
+    def own(self):
+        return pltpu.make_async_copy(self.rows_ref, self.target_ref, self.own_sem.at[0])
+
+    def away(self, part):
+        count = self.rows_ref.shape[0] // self.PARTS
+        at = slice(part * count, (part + 1) * count)
+        return pltpu.make_async_remote_copy(
+            src_ref=self.rows_ref.at[at, :],
+            dst_ref=self.target_ref.at[at, :],
+            send_sem=self.sem.at[0, part],
+            recv_sem=self.sem.at[1, part],
+            device_id=self.place.corner,
+            device_id_type=MESH,
+        )
 
     def start(self):
         @pl.when(self.place.stays)
         def _():
             self.own().start()
-            self.hand_own().start()
 
         @pl.when(jnp.logical_not(self.place.stays))
         def _():
-            self.away().start()
-
-    def step(self):
-        @pl.when(jnp.logical_not(self.place.stays))
-        def _():
-            self.away().wait()
-            self.hand_got().start()
-
-    def end(self):
+            for part in range(self.PARTS):
+                self.away(part).start()
+
+    def wait(self):
         @pl.when(self.place.stays)
         def _():
             self.own().wait()
 
-        self.hand_got().wait()
+        @pl.when(jnp.logical_not(self.place.stays))
+        def _():
+            for part in range(self.PARTS):
+                self.away(part).wait()
 
 
 class WeightGather:
@@ -1190,7 +1244,7 @@
     query, key, value, outer, up_a, up_b, down_a, down_b = range(8)
     gather = WeightGather(place, line, groups, scratch[19:22])
     tokens = RowSwap(place, tokens_ref, tokens_out, scratch[22:24])
-    grads = RowSwap(place, grads_ref, grads_out, scratch[24:26])
+    grads = CornerMove(place, grads_ref, grads_out, scratch[24:26])
 
     def load(group):
         if group < 3:
@@ -1299,26 +1353,27 @@
     gather.enter(key)
     gather.line_most(query)
     gather.line_start(key)
-    tokens.start()
+    tokens.start((0,))
     gather.line_end(query)
     gather.plane_start(query)
     gather.plane_step(down_b)
     gather.enter(value)
     gather.line_most(key)
     gather.line_start(value)
+    tokens.start((1,))
     gather.line_end(key)
     gather.plane_step(query)
     gather.plane_start(key)
     gather.plane_end(down_b)
     gather.line_most(value)
-    gather.line_end(value)
     gather.enter(outer)
     gather.line_start(outer)
+    tokens.start((2, 3))
+    gather.line_end(value)
     gather.plane_end(query)
     load(query).start()
     gather.plane_step(key)
     gather.plane_start(value)
-    tokens.step()
     fill_distance(seg_rows, seg_cols, distance)
     gather.enter(up_a)
     gather.line_most(outer)
@@ -1328,21 +1383,25 @@
     gather.line_end(outer)
     gather.plane_step(value)
     gather.plane_start(outer)
+    tokens.step()
+    gather.line_step(up_a, 1)
     tokens.end()
     x_load.start()
+    for step in range(2, line - 1):
+        gather.line_step(up_a, step)
+    gather.enter(up_b)
+    gather.line_start(up_b)
     x_load.wait()
     normalize_tokens()
     store(3).start()
-    gather.enter(up_b)
-    gather.line_most(up_a)
-    gather.line_start(up_b)
-    project(query)
-    gather.line_end(up_a)
-    gather.line_start(down_b)
     gather.plane_end(value)
     load(value).start()
+    gather.line_end(up_a)
     gather.plane_step(outer)
     gather.plane_start(up_a)
+    project(query)
+    gather.line_step(up_b, 1)
+    gather.line_start(down_b)
     project(key)
     project(value)
     store(0).start()
@@ -1350,7 +1409,8 @@
     def beside(index):
         if index == 0:
             gather.enter(down_a)
-            gather.line_most(up_b)
+            for step in range(2, line - 1):
+                gather.line_step(up_b, step)
             gather.line_start(down_a)
             gather.plane_end(outer)
             load(outer).start()
@@ -1381,12 +1441,12 @@
     gather.plane_step(up_b)
     gather.line_end(down_a)
     gather.plane_start(down_a)
+    for step in range(2, line - 1):
+        gather.line_step(down_b, step)
+    grads.start()
     lax.fori_loop(0, size // 256, add_branch, 0)
     store(4).start()
     store(5).start()
-    for step in range(2, line - 1):
-        gather.line_step(down_b, step)
-    grads.start()
     gather.plane_end(up_a)
     load(up_a).start()
     feed(0)
@@ -1395,9 +1455,8 @@
     load(up_b).start()
     feed(1)
     gather.line_end(down_b)
-    grads.step()
     gather.plane_end(down_a)
-    grads.end()
+    grads.wait()
     for index in range(len(pairs)):
         store(index).wait()
     for group in range(len(groups)):
@@ -1426,7 +1485,7 @@
         ((2, length, wide), low),
     ]
     outs = [(whole(3, narrow), low), (whole(1, narrow), low), (whole(2, wide), low), (whole(2, wide), low)]
-    outs += [((length, width), low)] * 2 + kept
+    outs += [((length, width), low), (grads.shape, low)] + kept
     held = [(length, width)] * 2 + [whole(3, narrow), whole(1, narrow), whole(2, wide)]
     results = pl.pallas_call(
         functools.partial(forward_kernel, line),
@@ -1440,7 +1499,8 @@
         + [pltpu.VMEM(*each) for each in kept[4:]]
         + [dma((8,)), dma((10,)), dma((length // 256,)), dma((length // 256,))]
         + WeightGather.scratch(8, line)
-        + RowSwap.scratch() * 2,
+        + RowSwap.scratch()
+        + CornerMove.scratch(),
         compiler_params=pltpu.CompilerParams(
             collective_id=1, has_side_effects=True, vmem_limit_bytes=62 * 1024 * 1024
         ),
@@ -1464,7 +1524,7 @@
     line, grads_ref, act_ref, bend_ref, down_ref, up_ref, hidden_ref, middle_ref, mixed_ref, out_ref, gain,
     down_home, up_out, out_out, mixed_out, mid_out, sums_out, hidden_sums,
     grads, act, pre, down, up, hidden, middle, mixed, weight, part, got, low, mid, down_v, out_v, mixed_v,
-    load_sem, store_sem, send_sem, recv_sem, *scratch
+    load_sem, store_sem, send_sem, recv_sem, give_sem, *scratch
 ):
     place = Place()
     bend, up_v = pre, down
@@ -1482,8 +1542,17 @@
     size = grads.shape[0]
     half = size // 2
     blocks = size // 256
+    own_rows = grads.at[pl.ds(pl.multiple_of(place.core * half, half), half), :]
+    give_rows = pltpu.make_async_remote_copy(
+        src_ref=grads_ref,
+        dst_ref=own_rows,
+        send_sem=give_sem.at[0],
+        recv_sem=give_sem.at[1],
+        device_id=place.twin,
+        device_id_type=MESH,
+    )
     sources = (
-        (grads_ref, grads), (down_ref, down), (bend_ref, bend), (up_ref, up), (act_ref.at[0], act.at[0]),
+        (grads_ref, own_rows), (down_ref, down), (bend_ref, bend), (up_ref, up), (act_ref.at[0], act.at[0]),
         (middle_ref, middle), (out_ref, weight), (hidden_ref, hidden), (mixed_ref, mixed),
     )
     load_g, load_down, load_bend, load_up, load_act, load_middle, load_out, load_hidden, load_mixed = (
@@ -1493,6 +1562,7 @@
     for each in (load_g, load_act, load_down, load_bend, load_up, load_more, load_middle, load_out, load_hidden, load_mixed):
         each.start()
     greet(place, line)
+    give_rows.start()
 
     def rows(index, count=256):
         return pl.ds(pl.multiple_of(index * count, count), count)
@@ -1572,6 +1642,7 @@
 
     hidden_sums[...] = jnp.zeros_like(hidden_sums)
     load_g.wait()
+    give_rows.wait()
     load_act.wait()
     down_gradient(0)
     one.plane.start()
@@ -1649,11 +1720,11 @@
         ],
         in_specs=[hbm] * 9 + [vmem],
         out_specs=[hbm] * 5 + [vmem] * 2,
-        scratch_shapes=[held(each) for each in (grads, act, bend, down, up, hidden, middle, mixed, out)]
+        scratch_shapes=[square] + [held(each) for each in (act, bend, down, up, hidden, middle, mixed, out)]
         + [square, square, square, pltpu.VMEM((size // 2, size), jnp.float32)]
         + [pltpu.VMEM((2, 2, 2, 2, rows, act.shape[2]), low)]
         + [pltpu.VMEM((1, size, narrow), low), pltpu.VMEM((size, narrow), low)]
-        + [dma((11,)), dma((6, size // 256)), dma((size // 256,)), dma((size // 256,))]
+        + [dma((11,)), dma((6, size // 256)), dma((size // 256,)), dma((size // 256,)), dma((2,))]
         + [GroupSum.scratch(1, rows, act.shape[2], line)] * 2,
         compiler_params=pltpu.CompilerParams(
             collective_id=4, has_side_effects=True, vmem_limit_bytes=62 * 1024 * 1024

time: 462 us -> 459 us (level)
    pallas_call x1, Pallas kernels: 142 us -> 136 us  [forward(): pl.pallas_call(functools.partial(forward_kernel, line), out_shape=[jax.Sh...]
where the time goes in v1:
time: 459 us; the launch traced here: 451 us
  Pallas kernels  426 us (93%)
  local copies, waits for them, and re-layouts  14.9 us (3%)
  other arithmetic  8.69 us (2%)
    pallas_call x1, Pallas kernels, forward(): pl.pallas_call(functools.partial(forward_kernel, line), out_shape=[jax.Sh...  136 us
    pallas_call x1, Pallas kernels, finish(): pl.pallas_call(functools.partial(finish_kernel, line), out_shape=[jax.Sha...  115 us
    pallas_call x1, Pallas kernels, attend_back(): pl.pallas_call(functools.partial(back_kernel, line), out_shape=[jax.Shape...  112 us
    pallas_call x1, Pallas kernels, middle_back(): pl.pallas_call(functools.partial(middle_kernel, line), out_shape=[jax.Sha...  63 us
  transfers between devices with their start and end apart: 1, of which 0 were waited for; matrix products, arithmetic and copies ran while one was open for 2% of the time, Pallas kernels for 0%

profile of v1, /device:TPU:0, one launch (start us, length us, event | category | flops | bytes accessed | tf_op | source)
XLA Modules:
  0.0 451.3 jit_solution(2146970956422203655)
XLA Ops:
  0.7 0.7 reshape.59
  1.9 1.6 fusion.8
  3.4 0.8 slice.40
  4.3 0.7 pad_maximum_fusion.qkv_bias
  5.0 0.6 fusion.4.slopes
  5.6 0.6 copy.33
  6.2 2.1 convert_element_type.16.mlp_ref
  8.3 1.8 convert_element_type.15.attn_ref
  10.1 1.0 copy.26.seg_rows
  11.1 136.2 %forward.1 = (bf16[3,2,2,2,128,512]{5,4,3,2,1,0:T(8,128)(2,1)}, bf16[1,2,2,2,128,512]{5,4,3,2,1,0:T(8,128)(2,1)}, bf16[2,2,2,2,128,1024]{5,4,3,2,1,0:T(8,128)(2,...) custom-call(bf16[4,128,256]{2,1,0:T(8,128)(2,1)} %convert_element_ty, ...), custom_call_target="tpu_custom_call" | custom-call | tf_op jit(solution)/shard_map/forward/pallas_call | solution.py:1490
  147.4 63.0 %middle_back.1 = (bf16[1,128,1024]{2,1,0:T(8,128)(2,1)}, bf16[2,1024,1024]{2,1,0:T(8,128)(2,1)}, bf16[1,1024,512]{2,1,0:T(8,128)(2,1)}, bf16[1024,512]{1,0:T(8,1...) custom-call(bf16[512,1024]{1,0:T(8,128)(2,1)} %get-tuple-element.40.grads_ref, ...), custom_call_target="tpu_custom_call" | custom-call | tf_op jit(solution)/shard_map/middle_back/pallas_call | solution.py:1710
  210.4 0.8 fusion.9
  211.2 0.7 slice.45
  211.9 111.8 %attend_back.1 = (bf16[4,128,256]{2,1,0:T(8,128)(2,1)}, bf16[1024,1024]{1,0:T(8,128)(2,1)}, f32[3,512]{1,0:T(4,128)}, f32[2,128,1024]{2,1,0:T(8,128)}, bf16[1024...) custom-call(bf16[2,2,2,2,128,1024]{5,4,3,2,1,0:T(8,128)(2,1)} %bitcast.44, bf16[1,2,2,2,128,512]{5,4,3,2,1,0:T(8,128)(2,1)} %bitcast.48, ...), custom_call_target="tpu_custom_call" | custom-call | tf_op jit(solution)/shard_map/attend_back/pallas_call | solution.py:1939
  323.7 0.8 slice_bitcast_fusion
  324.6 1.9 fusion.7
  326.5 1.3 concatenate.3.vec_ref
  327.8 115.0 %finish.1 = (f32[4,128,256]{2,1,0:T(8,128)}, f32[2,128,1024]{2,1,0:T(8,128)}, f32[16,1024]{1,0:T(8,128)}, f32[512,1024]{1,0:T(8,128)}, bf16[512,1024]{1,0:T(8,128)(2,1)}) custom-call(bf16[4,128,256]{2,1,0:T(8,128)(2,1)} %get-tuple-element.74.attn_ref, bf16[1024,2048]{1,0:T(8,128)(2,1)} %get-tuple-element.58.whole_ref, f32[16,1024]{1,0:T(8,128)} %concatenate.3.vec_ref, ...), custom_call_target="tpu_custom_call" | custom-call | tf_op jit(solution)/shard_map/finish/pallas_call | solution.py:2370
  442.8 1.6 multiply_subtract_fusion
  444.5 2.3 copy.45
  446.8 1.3 copy.46
  448.1 0.8 copy.47
  448.9 1.0 copy.48
  449.9 1.0 copy.49
  (36 shorter events, 0.8 us)
Async XLA Ops:
  1.4 8.7 %collective-permute-start = (s32[1024]{0:T(1024)S(1)}, s32[1024]{0:T(1024)S(1)}, u32[]{:S(2)}, u32[]{:S(2)}) collective-permute-start(s32[1024]{0:T(1024)S(1)} %bitcast.54), channel_id=1, source_target_pairs={{0,4},{1,5},{2,6},{3,7},{4,0},{5,1},{6,2},{7,3},{8,12},{9,13},{10,... | collective-permute-start | bytes 12296 | tf_op jit(solution)/shard_map/ppermute | solution.py:2438
  10.1 1.0 copy-start.7
  211.9 112.6 %copy-start.8 = (f32[2,1024]{1,0:T(2,128)S(1)}, f32[2,1024]{1,0:T(2,128)}, u32[]{:S(2)}) copy-start(f32[2,1024]{1,0:T(2,128)} %get-tuple-element.61) | copy-start | bytes 24580
  211.9 112.7 %copy-start.3 = (f32[4,128,256]{2,1,0:T(8,128)S(1)}, f32[4,128,256]{2,1,0:T(8,128)}, u32[]{:S(2)}) copy-start(f32[4,128,256]{2,1,0:T(8,128)} %param.15) | copy-start | bytes 1572868
  327.8 115.0 %copy-start.5 = (f32[12,1024]{1,0:T(8,128)S(1)}, f32[12,1024]{1,0:T(8,128)}, u32[]{:S(2)}) copy-start(f32[12,1024]{1,0:T(8,128)} %vectors.1) | copy-start | bytes 147460
  327.8 115.0 %copy-start.6 = (f32[12,1024]{1,0:T(8,128)S(1)}, f32[12,1024]{1,0:T(8,128)}, u32[]{:S(2)}) copy-start(f32[12,1024]{1,0:T(8,128)} %param.17) | copy-start | bytes 147460
  442.8 4.0 copy-start
  444.5 3.7 copy-start.4
  446.8 2.1 copy-start.1
  446.8 3.1 copy-start.2

commit v2 on v1

--- a/solution.py
+++ b/solution.py
@@ -874,7 +874,7 @@
         target[at] = total.astype(target.dtype)
         return carry
 
-    lax.fori_loop(0, math.prod(lead) * per, body, 0)
+    lax.fori_loop(0, math.prod(lead) * per, body, 0, unroll=4)
 
 
 class PlaneSum:
@@ -2122,6 +2122,93 @@
             sums[1] + jnp.sum(grad.reshape(fold), axis=0),
         )
 
+    def contract_rows(left, right):
+        return lax.dot_general(left, right, (((1,), (1,)), ((), ())), preferred_element_type=jnp.float32)
+
+    block = 256
+
+    def swap_block(slot, index):
+        return pltpu.make_async_remote_copy(
+            src_ref=sent.at[index],
+            dst_ref=got.at[slot, index],
+            send_sem=block_send.at[index],
+            recv_sem=block_recv.at[slot, index],
+            device_id=place.twin,
+            device_id_type=MESH,
+        )
+
+    def begin(matrix):
+        size, width = matrix.shape
+        pltpu.make_async_copy(matrix, matrix, start_sem.at[0]).wait()
+
+        def add_squares(step, total):
+            piece = matrix[pl.ds(pl.multiple_of(step * 32, 32), 32), :].astype(jnp.float32)
+            piece = piece * piece
+            return total + jnp.sum(piece.reshape(4, 8, width // 128, 128), axis=(0, 2))
+
+        squares = lax.fori_loop(0, size // 32, add_squares, jnp.zeros((8, 128), jnp.float32), unroll=4)
+        norm_own[...] = jnp.zeros((8, 128), jnp.float32) + jnp.sum(squares)
+        swap = pltpu.make_async_remote_copy(
+            src_ref=norm_own,
+            dst_ref=norm_got,
+            send_sem=norm_sem.at[0],
+            recv_sem=norm_sem.at[1],
+            device_id=place.twin,
+            device_id_type=MESH,
+        )
+        swap.start()
+        swap.wait()
+        scale = 1.0 / (jnp.sqrt(norm_own[...] + norm_got[...]) + 1e-06)
+        scale = scale[0:1, 0:1]
+
+        def scale_rows(step, carry):
+            at = pl.ds(pl.multiple_of(step * 32, 32), 32)
+            matrix[at, :] = (matrix[at, :].astype(jnp.float32) * scale).astype(jnp.bfloat16)
+            return carry
+
+        lax.fori_loop(0, size // 32, scale_rows, 0, unroll=4)
+
+    def iterate(matrix, repeat):
+        size, width = matrix.shape
+        blocks = size // block
+        slot = repeat % 2
+
+        def share(index, carry):
+            at = pl.ds(pl.multiple_of(index * block, block), block)
+            sent[index] = contract_rows(matrix[at, :], matrix[...]).astype(jnp.bfloat16)
+            swap_block(slot, index).start()
+            return carry
+
+        lax.fori_loop(0, blocks, share, 0)
+
+        def add(index, carry):
+            at = pl.ds(pl.multiple_of(index * block, block), block)
+            swap_block(slot, index).wait()
+            total = sent[index].astype(jnp.float32) + got[slot, index].astype(jnp.float32)
+            gram[at, :] = total.astype(jnp.bfloat16)
+            return carry
+
+        lax.fori_loop(0, blocks, add, 0)
+        square = jnp.dot(gram[...], gram[...], preferred_element_type=jnp.float32)
+        poly[...] = (coeff_b * gram[...].astype(jnp.float32) + coeff_c * square).astype(jnp.bfloat16)
+        step_width = min(width, 1024)
+
+        def advance(index, carry):
+            at = columns(index * step_width, step_width)
+            moved = jnp.dot(poly[...], matrix[:, at], preferred_element_type=jnp.float32)
+            matrix[:, at] = (coeff_a * matrix[:, at].astype(jnp.float32) + moved).astype(jnp.bfloat16)
+            return carry
+
+        lax.fori_loop(0, width // step_width, advance, 0)
+
+    @pl.when(owns_thin)
+    def _():
+        begin(thin)
+
+    @pl.when(owns_full)
+    def _():
+        begin(full)
+
     part_swap.wait()
     part_load.wait()
     tokens_load.wait()
@@ -2134,93 +2221,6 @@
     middle_load.wait()
     lax.fori_loop(0, half_rows // 32, out_rows, 0, unroll=2)
     when_moving(out_moves, lambda move: move.start())
-
-    def contract_rows(left, right):
-        return lax.dot_general(left, right, (((1,), (1,)), ((), ())), preferred_element_type=jnp.float32)
-
-    block = 256
-
-    def swap_block(slot, index):
-        return pltpu.make_async_remote_copy(
-            src_ref=sent.at[index],
-            dst_ref=got.at[slot, index],
-            send_sem=block_send.at[index],
-            recv_sem=block_recv.at[slot, index],
-            device_id=place.twin,
-            device_id_type=MESH,
-        )
-
-    def begin(matrix):
-        size, width = matrix.shape
-        pltpu.make_async_copy(matrix, matrix, start_sem.at[0]).wait()
-
-        def add_squares(step, total):
-            piece = matrix[pl.ds(pl.multiple_of(step * 32, 32), 32), :].astype(jnp.float32)
-            piece = piece * piece
-            return total + jnp.sum(piece.reshape(4, 8, width // 128, 128), axis=(0, 2))
-
-        squares = lax.fori_loop(0, size // 32, add_squares, jnp.zeros((8, 128), jnp.float32))
-        norm_own[...] = jnp.zeros((8, 128), jnp.float32) + jnp.sum(squares)
-        swap = pltpu.make_async_remote_copy(
-            src_ref=norm_own,
-            dst_ref=norm_got,
-            send_sem=norm_sem.at[0],
-            recv_sem=norm_sem.at[1],
-            device_id=place.twin,
-            device_id_type=MESH,
-        )
-        swap.start()
-        swap.wait()
-        scale = 1.0 / (jnp.sqrt(norm_own[...] + norm_got[...]) + 1e-06)
-        scale = scale[0:1, 0:1]
-
-        def scale_rows(step, carry):
-            at = pl.ds(pl.multiple_of(step * 32, 32), 32)
-            matrix[at, :] = (matrix[at, :].astype(jnp.float32) * scale).astype(jnp.bfloat16)
-            return carry
-
-        lax.fori_loop(0, size // 32, scale_rows, 0)
-
-    def iterate(matrix, repeat):
-        size, width = matrix.shape
-        blocks = size // block
-        slot = repeat % 2
-
-        def share(index, carry):
-            at = pl.ds(pl.multiple_of(index * block, block), block)
-            sent[index] = contract_rows(matrix[at, :], matrix[...]).astype(jnp.bfloat16)
-            swap_block(slot, index).start()
-            return carry
-
-        lax.fori_loop(0, blocks, share, 0)
-
-        def add(index, carry):
-            at = pl.ds(pl.multiple_of(index * block, block), block)
-            swap_block(slot, index).wait()
-            total = sent[index].astype(jnp.float32) + got[slot, index].astype(jnp.float32)
-            gram[at, :] = total.astype(jnp.bfloat16)
-            return carry
-
-        lax.fori_loop(0, blocks, add, 0)
-        square = jnp.dot(gram[...], gram[...], preferred_element_type=jnp.float32)
-        poly[...] = (coeff_b * gram[...].astype(jnp.float32) + coeff_c * square).astype(jnp.bfloat16)
-        step_width = min(width, 1024)
-
-        def advance(index, carry):
-            at = columns(index * step_width, step_width)
-            moved = jnp.dot(poly[...], matrix[:, at], preferred_element_type=jnp.float32)
-            matrix[:, at] = (coeff_a * matrix[:, at].astype(jnp.float32) + moved).astype(jnp.bfloat16)
-            return carry
-
-        lax.fori_loop(0, width // step_width, advance, 0)
-
-    @pl.when(owns_thin)
-    def _():
-        begin(thin)
-
-    @pl.when(owns_full)
-    def _():
-        begin(full)
 
     for repeat in range(NS_STEPS):
 

time: 459 us -> 455 us (level)
  no operation moved by 1% of the time
where the time goes in v2:
time: 455 us; the launch traced here: 447 us
  Pallas kernels  422 us (93%)
  local copies, waits for them, and re-layouts  14.9 us (3%)
  other arithmetic  8.69 us (2%)
    pallas_call x1, Pallas kernels, forward(): pl.pallas_call(functools.partial(forward_kernel, line), out_shape=[jax.Sh...  136 us
    pallas_call x1, Pallas kernels, finish(): pl.pallas_call(functools.partial(finish_kernel, line), out_shape=[jax.Sha...  114 us
    pallas_call x1, Pallas kernels, attend_back(): pl.pallas_call(functools.partial(back_kernel, line), out_shape=[jax.Shape...  109 us
    pallas_call x1, Pallas kernels, middle_back(): pl.pallas_call(functools.partial(middle_kernel, line), out_shape=[jax.Sha...  62.6 us
  transfers between devices with their start and end apart: 1, of which 0 were waited for; matrix products, arithmetic and copies ran while one was open for 2% of the time, Pallas kernels for 0%

profile of v2, /device:TPU:0, one launch (start us, length us, event | category | flops | bytes accessed | tf_op | source)
XLA Modules:
  0.0 447.3 jit_solution(4015446328351437195)
XLA Ops:
  0.7 0.7 reshape.59
  1.9 1.6 fusion.8
  3.4 0.8 slice.40
  4.3 0.7 pad_maximum_fusion.qkv_bias
  5.0 0.6 fusion.4.slopes
  5.6 0.6 copy.33
  6.2 2.1 convert_element_type.16.mlp_ref
  8.3 1.8 convert_element_type.15.attn_ref
  10.1 1.0 copy.26.seg_rows
  11.1 136.2 %forward.1 = (bf16[3,2,2,2,128,512]{5,4,3,2,1,0:T(8,128)(2,1)}, bf16[1,2,2,2,128,512]{5,4,3,2,1,0:T(8,128)(2,1)}, bf16[2,2,2,2,128,1024]{5,4,3,2,1,0:T(8,128)(2,...) custom-call(bf16[4,128,256]{2,1,0:T(8,128)(2,1)} %convert_element_ty, ...), custom_call_target="tpu_custom_call" | custom-call | tf_op jit(solution)/shard_map/forward/pallas_call | solution.py:1490
  147.4 62.6 %middle_back.1 = (bf16[1,128,1024]{2,1,0:T(8,128)(2,1)}, bf16[2,1024,1024]{2,1,0:T(8,128)(2,1)}, bf16[1,1024,512]{2,1,0:T(8,128)(2,1)}, bf16[1024,512]{1,0:T(8,1...) custom-call(bf16[512,1024]{1,0:T(8,128)(2,1)} %get-tuple-element.40.grads_ref, ...), custom_call_target="tpu_custom_call" | custom-call | tf_op jit(solution)/shard_map/middle_back/pallas_call | solution.py:1710
  210.0 0.8 fusion.9
  210.8 0.7 slice.45
  211.5 109.3 %attend_back.1 = (bf16[4,128,256]{2,1,0:T(8,128)(2,1)}, bf16[1024,1024]{1,0:T(8,128)(2,1)}, f32[3,512]{1,0:T(4,128)}, f32[2,128,1024]{2,1,0:T(8,128)}, bf16[1024...) custom-call(bf16[2,2,2,2,128,1024]{5,4,3,2,1,0:T(8,128)(2,1)} %bitcast.44, bf16[1,2,2,2,128,512]{5,4,3,2,1,0:T(8,128)(2,1)} %bitcast.48, ...), custom_call_target="tpu_custom_call" | custom-call | tf_op jit(solution)/shard_map/attend_back/pallas_call | solution.py:1939
  320.8 0.8 slice_bitcast_fusion
  321.7 1.9 fusion.7
  323.6 1.3 concatenate.3.vec_ref
  324.9 113.8 %finish.1 = (f32[4,128,256]{2,1,0:T(8,128)}, f32[2,128,1024]{2,1,0:T(8,128)}, f32[16,1024]{1,0:T(8,128)}, f32[512,1024]{1,0:T(8,128)}, bf16[512,1024]{1,0:T(8,128)(2,1)}) custom-call(bf16[4,128,256]{2,1,0:T(8,128)(2,1)} %get-tuple-element.74.attn_ref, bf16[1024,2048]{1,0:T(8,128)(2,1)} %get-tuple-element.58.whole_ref, f32[16,1024]{1,0:T(8,128)} %concatenate.3.vec_ref, ...), custom_call_target="tpu_custom_call" | custom-call | tf_op jit(solution)/shard_map/finish/pallas_call | solution.py:2370
  438.8 1.6 multiply_subtract_fusion
  440.4 2.3 copy.45
  442.8 1.3 copy.46
  444.1 0.8 copy.47
  444.9 1.0 copy.48
  445.8 1.0 copy.49
  (36 shorter events, 0.8 us)
Async XLA Ops:
  1.4 8.7 %collective-permute-start = (s32[1024]{0:T(1024)S(1)}, s32[1024]{0:T(1024)S(1)}, u32[]{:S(2)}, u32[]{:S(2)}) collective-permute-start(s32[1024]{0:T(1024)S(1)} %bitcast.54), channel_id=1, source_target_pairs={{0,4},{1,5},{2,6},{3,7},{4,0},{5,1},{6,2},{7,3},{8,12},{9,13},{10,... | collective-permute-start | bytes 12296 | tf_op jit(solution)/shard_map/ppermute | solution.py:2438
  10.1 1.0 copy-start.7
  211.5 110.1 %copy-start.8 = (f32[2,1024]{1,0:T(2,128)S(1)}, f32[2,1024]{1,0:T(2,128)}, u32[]{:S(2)}) copy-start(f32[2,1024]{1,0:T(2,128)} %get-tuple-element.61) | copy-start | bytes 24580
  211.5 110.2 %copy-start.3 = (f32[4,128,256]{2,1,0:T(8,128)S(1)}, f32[4,128,256]{2,1,0:T(8,128)}, u32[]{:S(2)}) copy-start(f32[4,128,256]{2,1,0:T(8,128)} %param.15) | copy-start | bytes 1572868
  324.9 113.8 %copy-start.5 = (f32[12,1024]{1,0:T(8,128)S(1)}, f32[12,1024]{1,0:T(8,128)}, u32[]{:S(2)}) copy-start(f32[12,1024]{1,0:T(8,128)} %vectors.1) | copy-start | bytes 147460
  324.9 113.8 %copy-start.6 = (f32[12,1024]{1,0:T(8,128)S(1)}, f32[12,1024]{1,0:T(8,128)}, u32[]{:S(2)}) copy-start(f32[12,1024]{1,0:T(8,128)} %param.17) | copy-start | bytes 147460
  438.7 4.0 copy-start
  440.4 3.7 copy-start.4
  442.8 2.1 copy-start.1
  442.8 3.1 copy-start.2

commit v3 on v2

--- a/solution.py
+++ b/solution.py
@@ -2129,8 +2129,8 @@
 
     def swap_block(slot, index):
         return pltpu.make_async_remote_copy(
-            src_ref=sent.at[index],
-            dst_ref=got.at[slot, index],
+            src_ref=sent.at[index, :, index * block :],
+            dst_ref=got.at[slot, index, :, index * block :],
             send_sem=block_send.at[index],
             recv_sem=block_recv.at[slot, index],
             device_id=place.twin,
@@ -2173,22 +2173,19 @@
         blocks = size // block
         slot = repeat % 2
 
-        def share(index, carry):
-            at = pl.ds(pl.multiple_of(index * block, block), block)
-            sent[index] = contract_rows(matrix[at, :], matrix[...]).astype(jnp.bfloat16)
+        for index in range(blocks):
+            at = slice(index * block, (index + 1) * block)
+            sent[index, :, index * block :] = contract_rows(matrix[at, :], matrix[index * block :, :]).astype(jnp.bfloat16)
             swap_block(slot, index).start()
-            return carry
-
-        lax.fori_loop(0, blocks, share, 0)
-
-        def add(index, carry):
-            at = pl.ds(pl.multiple_of(index * block, block), block)
+        for index in range(blocks):
+            at = slice(index * block, (index + 1) * block)
             swap_block(slot, index).wait()
-            total = sent[index].astype(jnp.float32) + got[slot, index].astype(jnp.float32)
-            gram[at, :] = total.astype(jnp.bfloat16)
-            return carry
-
-        lax.fori_loop(0, blocks, add, 0)
+            total = sent[index, :, index * block :].astype(jnp.float32)
+            total = (total + got[slot, index, :, index * block :].astype(jnp.float32)).astype(jnp.bfloat16)
+            gram[at, index * block :] = total
+            if index < blocks - 1:
+                gram[(index + 1) * block :, at] = total[:, block:].T
+
         square = jnp.dot(gram[...], gram[...], preferred_element_type=jnp.float32)
         poly[...] = (coeff_b * gram[...].astype(jnp.float32) + coeff_c * square).astype(jnp.bfloat16)
         step_width = min(width, 1024)

time: 455 us -> 447 us (0.982)
  Pallas kernels: 422 us -> 414 us
    pallas_call x1, Pallas kernels: 114 us -> 106 us  [finish(): pl.pallas_call(functools.partial(finish_kernel, line), out_shape=[jax.Sha...]
where the time goes in v3:
time: 447 us; the launch traced here: 439 us
  Pallas kernels  414 us (93%)
  local copies, waits for them, and re-layouts  14.9 us (3%)
  other arithmetic  8.69 us (2%)
    pallas_call x1, Pallas kernels, forward(): pl.pallas_call(functools.partial(forward_kernel, line), out_shape=[jax.Sh...  136 us
    pallas_call x1, Pallas kernels, attend_back(): pl.pallas_call(functools.partial(back_kernel, line), out_shape=[jax.Shape...  109 us
    pallas_call x1, Pallas kernels, finish(): pl.pallas_call(functools.partial(finish_kernel, line), out_shape=[jax.Sha...  106 us
    pallas_call x1, Pallas kernels, middle_back(): pl.pallas_call(functools.partial(middle_kernel, line), out_shape=[jax.Sha...  62.8 us
  transfers between devices with their start and end apart: 1, of which 0 were waited for; matrix products, arithmetic and copies ran while one was open for 2% of the time, Pallas kernels for 0%

profile of v3, /device:TPU:0, one launch (start us, length us, event | category | flops | bytes accessed | tf_op | source)
XLA Modules:
  0.0 439.2 jit_solution(4848763453581532827)
XLA Ops:
  0.7 0.7 reshape.59
  1.9 1.6 fusion.8
  3.4 0.8 slice.40
  4.3 0.7 pad_maximum_fusion.qkv_bias
  5.0 0.6 fusion.4.slopes
  5.6 0.6 copy.33
  6.2 2.1 convert_element_type.16.mlp_ref
  8.3 1.8 convert_element_type.15.attn_ref
  10.1 1.0 copy.26.seg_rows
  11.1 136.2 %forward.1 = (bf16[3,2,2,2,128,512]{5,4,3,2,1,0:T(8,128)(2,1)}, bf16[1,2,2,2,128,512]{5,4,3,2,1,0:T(8,128)(2,1)}, bf16[2,2,2,2,128,1024]{5,4,3,2,1,0:T(8,128)(2,...) custom-call(bf16[4,128,256]{2,1,0:T(8,128)(2,1)} %convert_element_ty, ...), custom_call_target="tpu_custom_call" | custom-call | tf_op jit(solution)/shard_map/forward/pallas_call | solution.py:1490
  147.4 62.8 %middle_back.1 = (bf16[1,128,1024]{2,1,0:T(8,128)(2,1)}, bf16[2,1024,1024]{2,1,0:T(8,128)(2,1)}, bf16[1,1024,512]{2,1,0:T(8,128)(2,1)}, bf16[1024,512]{1,0:T(8,1...) custom-call(bf16[512,1024]{1,0:T(8,128)(2,1)} %get-tuple-element.40.grads_ref, ...), custom_call_target="tpu_custom_call" | custom-call | tf_op jit(solution)/shard_map/middle_back/pallas_call | solution.py:1710
  210.1 0.8 fusion.9
  211.0 0.7 slice.45
  211.7 109.3 %attend_back.1 = (bf16[4,128,256]{2,1,0:T(8,128)(2,1)}, bf16[1024,1024]{1,0:T(8,128)(2,1)}, f32[3,512]{1,0:T(4,128)}, f32[2,128,1024]{2,1,0:T(8,128)}, bf16[1024...) custom-call(bf16[2,2,2,2,128,1024]{5,4,3,2,1,0:T(8,128)(2,1)} %bitcast.44, bf16[1,2,2,2,128,512]{5,4,3,2,1,0:T(8,128)(2,1)} %bitcast.48, ...), custom_call_target="tpu_custom_call" | custom-call | tf_op jit(solution)/shard_map/attend_back/pallas_call | solution.py:1939
  321.0 0.8 slice_bitcast_fusion
  321.9 1.9 fusion.7
  323.8 1.3 concatenate.3.vec_ref
  325.1 105.5 %finish.1 = (f32[4,128,256]{2,1,0:T(8,128)}, f32[2,128,1024]{2,1,0:T(8,128)}, f32[16,1024]{1,0:T(8,128)}, f32[512,1024]{1,0:T(8,128)}, bf16[512,1024]{1,0:T(8,128)(2,1)}) custom-call(bf16[4,128,256]{2,1,0:T(8,128)(2,1)} %get-tuple-element.74.attn_ref, bf16[1024,2048]{1,0:T(8,128)(2,1)} %get-tuple-element.58.whole_ref, f32[16,1024]{1,0:T(8,128)} %concatenate.3.vec_ref, ...), custom_call_target="tpu_custom_call" | custom-call | tf_op jit(solution)/shard_map/finish/pallas_call | solution.py:2367
  430.7 1.6 multiply_subtract_fusion
  432.3 2.3 copy.45
  434.7 1.3 copy.46
  436.0 0.8 copy.47
  436.8 1.0 copy.48
  437.8 1.0 copy.49
  (36 shorter events, 0.8 us)
Async XLA Ops:
  1.4 8.7 %collective-permute-start = (s32[1024]{0:T(1024)S(1)}, s32[1024]{0:T(1024)S(1)}, u32[]{:S(2)}, u32[]{:S(2)}) collective-permute-start(s32[1024]{0:T(1024)S(1)} %bitcast.54), channel_id=1, source_target_pairs={{0,4},{1,5},{2,6},{3,7},{4,0},{5,1},{6,2},{7,3},{8,12},{9,13},{10,... | collective-permute-start | bytes 12296 | tf_op jit(solution)/shard_map/ppermute | solution.py:2435
  10.1 1.0 copy-start.7
  211.7 110.1 %copy-start.8 = (f32[2,1024]{1,0:T(2,128)S(1)}, f32[2,1024]{1,0:T(2,128)}, u32[]{:S(2)}) copy-start(f32[2,1024]{1,0:T(2,128)} %get-tuple-element.61) | copy-start | bytes 24580
  211.7 110.3 %copy-start.3 = (f32[4,128,256]{2,1,0:T(8,128)S(1)}, f32[4,128,256]{2,1,0:T(8,128)}, u32[]{:S(2)}) copy-start(f32[4,128,256]{2,1,0:T(8,128)} %param.15) | copy-start | bytes 1572868
  325.1 105.5 %copy-start.5 = (f32[12,1024]{1,0:T(8,128)S(1)}, f32[12,1024]{1,0:T(8,128)}, u32[]{:S(2)}) copy-start(f32[12,1024]{1,0:T(8,128)} %vectors.1) | copy-start | bytes 147460
  325.1 105.5 %copy-start.6 = (f32[12,1024]{1,0:T(8,128)S(1)}, f32[12,1024]{1,0:T(8,128)}, u32[]{:S(2)}) copy-start(f32[12,1024]{1,0:T(8,128)} %param.17) | copy-start | bytes 147460
  430.7 4.0 copy-start
  432.3 3.7 copy-start.4
  434.7 2.1 copy-start.1
  434.7 3.1 copy-start.2
